TPU v7x, 128 devices: a whole 4x4x4 slice. The times are simulated.
128 devices in a mesh: seq: 16 (over x, y), head: 8 (over z, core).
Axes of the slice: x: 4, y: 4, z: 4, core: 2. Of those that a mesh axis runs over, the one named last changes fastest.
Arguments:
- queries: bfloat16 [16384, 4096], P(('seq', 'head')), may hold values from -6 to 6
- keys: bfloat16 [16384, 4096], P(('seq', 'head')), may hold values from -6 to 6
- values: bfloat16 [16384, 4096], P(('seq', 'head')), may hold values from -6 to 6
- beta: bfloat16 [16384, 32], P(('seq', 'head')), may hold values from 0 to 1
- log_decay: bfloat16 [16384, 32], P(('seq', 'head')), may hold values from -1 to 0
- seg_lengths: int32 [8], replicated, may hold values from 1 to 12288, 16384 in all
Outputs:
- mixed: bfloat16 [16384, 4096], P(('seq', 'head'))
All inputs are finite; a program needn't handle non-finite values.
Results may differ from a plain program's by a relative error of at most 0.0017.
Values may be sent and summed in bfloat16 or wider, within the bound.
No kernel may reach another device: no remote copies, remote signals or barrier semaphores. Data moves between devices by JAX's collectives and lax.ppermute only.
A program may use at most 128 MiB of HBM per device.

v0:
```python
from functools import partial

import jax
import jax.numpy as jnp
from jax import lax
from jax.sharding import PartitionSpec as P

DK = 128
DV = 128
SPAN = 64


def span_parts(query_rows, key_rows, value_rows, write_rate, log_gate, reset_flags, inclusive):
    highest = lax.Precision.HIGHEST
    block_rows = query_rows.shape[0]
    log_level = jnp.cumsum(log_gate)
    region = jnp.cumsum(reset_flags)
    row_indices = jnp.arange(block_rows)[:, None]
    col_ids = jnp.arange(block_rows)[None, :]
    inside_segment_mask = (col_ids <= row_indices) & (region[:, None] == region[None, :])
    log_gap = jnp.where(inside_segment_mask, log_level[:, None] - log_level[None, :], 0.0)
    weight = jnp.where(inside_segment_mask, jnp.exp(log_gap), 0.0)
    carried = jnp.where(region == 0, jnp.exp(log_level), 0.0)
    strictly = col_ids < row_indices
    intersection = jnp.dot(key_rows, key_rows.T, precision=highest)
    system = jnp.eye(block_rows, dtype=query_rows.dtype) + jnp.where(
        strictly, write_rate[:, None] * weight * intersection, 0.0
    )
    right_side = jnp.concatenate(
        [write_rate[:, None] * value_rows, (write_rate * carried)[:, None] * key_rows], axis=1
    )
    solved = jax.scipy.linalg.solve_triangular(system, right_side, lower=True, unit_diagonal=True)
    value_width = value_rows.shape[1]
    update = solved[:, :value_width]
    shrink = solved[:, value_width:]
    scores = jnp.dot(query_rows, key_rows.T, precision=highest) * weight
    if not inclusive:
        scores = jnp.where(strictly, scores, 0.0)
    local_out = jnp.dot(scores, update, precision=highest)
    effective = carried[:, None] * query_rows - jnp.dot(scores, shrink, precision=highest)
    trailing_weight = weight[block_rows - 1]
    scaled = trailing_weight[:, None] * key_rows
    transit = carried[block_rows - 1] * jnp.eye(
        key_rows.shape[1], dtype=query_rows.dtype
    ) - jnp.dot(shrink.T, scaled, precision=highest)
    inject = jnp.dot(update.T, scaled, precision=highest)
    return (local_out, effective, transit, inject)


def block_pieces(query_rows, key_rows, value_rows, write_rate, log_gate, reset_flags, inclusive):
    count = query_rows.shape[0] // SPAN

    def split(member):
        return member.reshape((count, SPAN) + member.shape[1:])

    return jax.vmap(partial(span_parts, inclusive=inclusive))(
        split(query_rows),
        split(key_rows),
        split(value_rows),
        split(write_rate),
        split(log_gate),
        split(reset_flags),
    )


def combine(earlier, later):
    highest = lax.Precision.HIGHEST
    return (
        jnp.einsum("hij,hjk->hik", earlier[0], later[0], precision=highest),
        jnp.einsum("hij,hjk->hik", earlier[1], later[0], precision=highest) + later[1],
    )


def summarize(transit, inject):
    heads = transit.shape[0]
    start = (
        jnp.broadcast_to(jnp.eye(DK, dtype=jnp.float32), (heads, DK, DK)),
        jnp.zeros((heads, DV, DK), jnp.float32),
    )

    def step(carry, piece):
        return (combine(carry, piece), None)

    result, unused = lax.scan(
        step, start, (jnp.moveaxis(transit, 1, 0), jnp.moveaxis(inject, 1, 0))
    )
    return result


def emit(local_out, effective, transit, inject, state):
    highest = lax.Precision.HIGHEST
    moved = (
        jnp.moveaxis(local_out, 1, 0),
        jnp.moveaxis(effective, 1, 0),
        jnp.moveaxis(transit, 1, 0),
        jnp.moveaxis(inject, 1, 0),
    )

    def step(carry, piece):
        out_block, effect_rows, transit_step, inject_step = piece
        produced = out_block + jnp.einsum("hck,hvk->hcv", effect_rows, carry, precision=highest)
        carry = jnp.einsum("hvj,hjk->hvk", carry, transit_step, precision=highest) + inject_step
        return (carry, produced)

    final_state, produced = lax.scan(step, state, moved)
    heads = produced.shape[1]
    return jnp.moveaxis(produced, 0, 1).reshape(heads, -1, produced.shape[-1])


def on_device(queries, keys, values, beta, log_decay, seg_lengths):
    highest = lax.Precision.HIGHEST
    query_all, key_all, value_all, rate_all, gate_values_full = (
        lax.all_to_all(queries, "head", split_axis=1, concat_axis=0, tiled=True),
        lax.all_to_all(keys, "head", split_axis=1, concat_axis=0, tiled=True),
        lax.all_to_all(values, "head", split_axis=1, concat_axis=0, tiled=True),
        lax.all_to_all(beta, "head", split_axis=1, concat_axis=0, tiled=True),
        lax.all_to_all(log_decay, "head", split_axis=1, concat_axis=0, tiled=True),
    )
    rows = query_all.shape[0]
    heads = rate_all.shape[1]
    spread = lax.axis_size("seq")
    place = lax.axis_index("seq")
    total = rows * spread
    starts = jnp.cumsum(seg_lengths) - seg_lengths
    positions = place * rows + jnp.arange(rows, dtype=jnp.int32)
    forward_reset = jnp.any(positions[:, None] == starts[None, :], axis=1).astype(jnp.int32)
    backward_reset = (
        jnp.any((positions + 1)[:, None] == starts[None, :], axis=1) | (positions == total - 1)
    ).astype(jnp.int32)

    def by_head(array, width):
        return array.reshape(rows, heads, width).transpose(1, 0, 2).astype(jnp.float32)

    query_heads = by_head(query_all, DK)
    key_raw = by_head(key_all, DK)
    key_heads = key_raw / jnp.sqrt(jnp.sum(key_raw * key_raw, axis=-1, keepdims=True) + 1e-06)
    value_heads = by_head(value_all, DV)
    rate_heads = rate_all.T.astype(jnp.float32)
    gate_heads = gate_values_full.T.astype(jnp.float32)
    forward_pieces = jax.vmap(partial(block_pieces, reset_flags=forward_reset, inclusive=True))(
        query_heads, key_heads, value_heads, rate_heads, gate_heads
    )
    backward_pieces = jax.vmap(
        partial(block_pieces, reset_flags=backward_reset[::-1], inclusive=False)
    )(
        query_heads[:, ::-1],
        key_heads[:, ::-1],
        value_heads[:, ::-1],
        rate_heads[:, ::-1],
        gate_heads[:, ::-1],
    )
    forward_sum = summarize(forward_pieces[2], forward_pieces[3])
    backward_sum = summarize(backward_pieces[2], backward_pieces[3])
    every = (
        lax.all_gather(forward_sum[0][None], "seq", axis=0, tiled=True),
        lax.all_gather(forward_sum[1][None], "seq", axis=0, tiled=True),
        lax.all_gather(backward_sum[0][None], "seq", axis=0, tiled=True),
        lax.all_gather(backward_sum[1][None], "seq", axis=0, tiled=True),
    )
    empty = jnp.zeros_like(forward_sum[1])

    def take_lower(step, state):
        moved = (
            jnp.einsum("hvj,hjk->hvk", state, every[0][step], precision=highest) + every[1][step]
        )
        return jnp.where(step < place, moved, state)

    def take_upper(step, state):
        source = spread - 1 - step
        moved = (
            jnp.einsum("hvj,hjk->hvk", state, every[2][source], precision=highest)
            + every[3][source]
        )
        return jnp.where(source > place, moved, state)

    forward_in = lax.fori_loop(0, spread, take_lower, empty)
    backward_in = lax.fori_loop(0, spread, take_upper, empty)
    forward_out = emit(
        forward_pieces[0], forward_pieces[1], forward_pieces[2], forward_pieces[3], forward_in
    )
    backward_out = emit(
        backward_pieces[0], backward_pieces[1], backward_pieces[2], backward_pieces[3], backward_in
    )[:, ::-1]
    mixed = (
        (forward_out + backward_out)
        .transpose(1, 0, 2)
        .reshape(rows, heads * DV)
        .astype(jnp.bfloat16)
    )
    return lax.all_to_all(mixed, "head", split_axis=0, concat_axis=1, tiled=True)


def solution(mesh):
    in_specs = (
        P(("seq", "head"), None),
        P(("seq", "head"), None),
        P(("seq", "head"), None),
        P(("seq", "head"), None),
        P(("seq", "head"), None),
        P(),
    )
    out_specs = P(("seq", "head"), None)
    return jax.shard_map(
        on_device, mesh=mesh, in_specs=in_specs, out_specs=out_specs, check_vma=False
    )
```

profile of v0, /device:TPU:1, one launch (start us, length us, event | category | flops | bytes accessed | tf_op | source)
XLA Modules:
  0.0 1230.6 jit_solution(14240629049935979253)
XLA Ops:
  6.5 6.9 all-to-all-start
  32.7 13.2 %all-to-all-done.2 = bf16[128,8,512]{0,2,1:T(8,128)(2,1)S(1)} async-done(((bf16[128,8,512]{0,2,1:T(8,128)(2,1)}), bf16[128,8,512]{0,2,1:T(8,128)(2,1)S(1)}, u32[]{:S(2)}, u32[]{:S(2)}) %all-to-all-start.2) | async-done | bytes 1048608 | tf_op jit(solution)/shard_map/all_to_all | solution.py:114
  64.3 316.0 %custom-call.8 = f32[4,16,1,64,64]{3,4,2,1,0:T(8,128)} custom-call(f32[4,16,1,64,64]{4,3,2,1,0:T(8,128)} %add_bitcast_fusion.1), custom_call_target="InvertDiagBlocksLowerTriangular" | custom-call | tf_op jit(solution)/shard_map/vmap(vmap(jit(_solve_triangular)))/triangular_solve | solution.py:32
  398.3 9.2 convolution_bitcast_fusion.9
  407.5 9.5 bitcast_subtract_fusion.1
  417.1 5.3 copy.192
  422.4 5.4 copy.193
  427.8 45.7 %while.82 = (s32[]{:T(128)}, f32[4,128,128]{1,2,0:T(8,128)S(1)}, f32[4,128,128]{1,2,0:T(8,128)S(1)}, f32[16,4,128,128]{2,3,1,0:T(8,128)}, f32[16,4,128,128]{2,3,1,0:T(8,128)}, /*index=5*/s32[]{:T(128)}, s32[]{:T(128)}) while((s32[]{:T(128)}, f32[4,128,128]{1,2,0:T(8,128)S(1)}, f32[4,128,128]{1,2,0:T(8,128)S(1)}, ...), condition=%wide.region_6.8_spmd.clone, body=%wide.region_5.7_spmd.clone.sunk | while | flops 201457664 | bytes 2885207 | solution.py:84
  478.3 11.8 rev.24
  490.1 17.6 %rev.25 = f32[4,1024,128]{1,2,0:T(8,128)} reverse(f32[4,1024,128]{1,2,0:T(8,128)} %bitcast.301), dimensions={1} | reverse | bytes 4194304 | tf_op jit(solution)/shard_map/rev | solution.py:148
  515.4 316.0 %custom-call.9 = f32[4,16,1,64,64]{3,4,2,1,0:T(8,128)} custom-call(f32[4,16,1,64,64]{4,3,2,1,0:T(8,128)} %add_bitcast_fusion), custom_call_target="InvertDiagBlocksLowerTriangular" | custom-call | tf_op jit(solution)/shard_map/vmap(vmap(jit(_solve_triangular)))/triangular_solve | solution.py:32
  843.4 9.6 bitcast_subtract_fusion
  853.0 5.4 copy.211
  858.4 10.2 convolution_bitcast_fusion.8
  868.6 5.4 copy.212
  874.1 45.9 %while.84 = (s32[]{:T(128)}, f32[4,128,128]{1,2,0:T(8,128)S(1)}, f32[4,128,128]{1,2,0:T(8,128)S(1)}, f32[16,4,128,128]{2,3,1,0:T(8,128)}, f32[16,4,128,128]{2,3,1,0:T(8,128)}, /*index=5*/s32[]{:T(128)}, s32[]{:T(128)}) while((s32[]{:T(128)}, f32[4,128,128]{1,2,0:T(8,128)S(1)}, f32[4,128,128]{1,2,0:T(8,128)S(1)}, ...), condition=%wide.region_15.17_spmd.clone, body=%wide.region_14.16_spmd.clone.sunk | while | flops 201457664 | bytes 2885207 | solution.py:84
  927.8 15.2 %all-to-all-done.4 = bf16[128,8,512]{0,2,1:T(8,128)(2,1)} async-done(((bf16[128,8,512]{0,2,1:T(8,128)(2,1)}), bf16[128,8,512]{0,2,1:T(8,128)(2,1)}, u32[]{:S(2)}, u32[]{:S(2)}) %all-to-all-start.4) | async-done | bytes 1048608 | tf_op jit(solution)/shard_map/all_to_all | solution.py:113
  953.9 17.6 %rev.26 = f32[4,1024,128]{1,2,0:T(8,128)} reverse(f32[4,1024,128]{1,2,0:T(8,128)} %bitcast_convert_fusion), dimensions={1} | reverse | bytes 4194304 | tf_op jit(solution)/shard_map/rev | solution.py:146
  1000.3 43.6 %while.83 = (s32[]{:T(128)}, f32[4,128,128]{1,2,0:T(8,128)S(1)}, s32[]{:T(128)}, f32[16,4,128,128]{3,2,1,0:T(8,128)}, f32[16,4,128,128]{3,2,1,0:T(8,128)}, /*index=5*/s32[]{:T(128)}, s32[]{:T(128)}) while((s32[]{:T(128)}, f32[4,128,128]{1,2,0:T(8,128)S(1)}, s32[]{:T(128)}, f32[16,4,128,128]{3,2,1,0:T(8,128)}, ...), condition=%wide.region_8.10_spmd.clone, body=%wide.region_7.9_spmd.clone.sunk | while | flops 100925440 | bytes 2885731 | solution.py:176
  1045.5 55.6 %while.80 = (s32[]{:T(128)}, f32[4,128,128]{1,2,0:T(8,128)S(1)}, f32[16,4,64,128]{3,2,0,1:T(8,128)}, f32[16,4,128,128]{2,3,1,0:T(8,128)}, f32[16,4,128,128]{2,3,...) while((s32[]{:T(128)}, f32[4,128,128]{1,2,0:T(8,128)S(1)}, ...), condition=%wide.region_10.12_spmd, body=%wide.region_9.11_spmd.sunk | while | flops 151093248 | bytes 2230357 | solution.py:105
  1101.2 43.9 %while.85 = (s32[]{:T(128)}, f32[4,128,128]{1,2,0:T(8,128)S(1)}, s32[]{:T(128)}, f32[16,4,128,128]{3,2,1,0:T(8,128)}, f32[16,4,128,128]{3,2,1,0:T(8,128)}, /*index=5*/s32[]{:T(128)}, s32[]{:T(128)}, s32[]{:T(128)}, s32[]{:T(128)}) while((s32[]{:T(128)}, f32[4,128,128]{1,2,0:T(8,128)S(1)}, s32[]{:T(128)}, ...), condition=%wide.region_17.19_spmd.clone, body=%wide.region_16.18_spmd.clone.sunk | while | flops 100925448 | bytes 2885793 | solution.py:177
  1145.3 45.2 %while.81 = (s32[]{:T(128)}, f32[4,128,128]{1,2,0:T(8,128)S(1)}, f32[16,4,64,128]{3,2,0,1:T(8,128)S(1)}, f32[16,4,128,128]{2,3,1,0:T(8,128)}, f32[16,4,128,128]{...) while((s32[]{:T(128)}, f32[4,128,128]{1,2,0:T(8,128)S(1)}, ...), condition=%wide.region_19.21_spmd, body=%wide.region_18.20_spmd.sunk | while | flops 151093248 | bytes 2230357 | solution.py:105
  1190.5 10.2 rev.27
  1204.1 18.4 %all_to_all.84 = bf16[8,128,512]{1,2,0:T(8,128)(2,1)S(1)} all-to-all(bf16[8,128,512]{1,2,0:T(8,128)(2,1)S(1)} %copy.225), channel_id=1, replica_groups=mesh['seq'=16,'head'=8] {'head'}, dimensions={0} | all-to-all | bytes 2097152 | tf_op jit(solution)/shard_map/all_to_all | solution.py:190
  (496 shorter events, 409.3 us)
Async XLA Ops:
  6.5 17.8 %copy-start.12 = (bf16[128,4096]{1,0:T(8,128)(2,1)S(1)}, bf16[128,4096]{1,0:T(8,128)(2,1)}, u32[]{:S(2)}) copy-start(bf16[128,4096]{1,0:T(8,128)(2,1)} %param.22) | copy-start | bytes 3145732
  6.5 11.6 all-to-all-start
  15.9 43.4 %copy-start.15 = (pred[64,64]{1,0:T(8,128)(4,1)}, pred[64,64]{1,0:T(8,128)(4,1)S(1)}, u32[]{:S(2)}) copy-start(pred[64,64]{1,0:T(8,128)(4,1)S(1)} %get-tuple-element.660) | copy-start | bytes 12292
  16.3 43.1 %copy-start.13 = (f32[64,64]{1,0:T(8,128)}, f32[64,64]{1,0:T(8,128)S(1)}, u32[]{:S(2)}) copy-start(f32[64,64]{1,0:T(8,128)S(1)} %get-tuple-element.663) | copy-start | bytes 49156
  18.1 8.6 all-to-all-start.1
  26.7 19.3 %all-to-all-start.2 = ((bf16[128,8,512]{0,2,1:T(8,128)(2,1)}), bf16[128,8,512]{0,2,1:T(8,128)(2,1)S(1)}, u32[]{:S(2)}, u32[]{:S(2)}) async-start(bf16[128,8,512]{0,2,1:T(8,128)(2,1)} %bitcast.23), calls=%async_computation.2 | async-start | bytes 2097152 | tf_op jit(solution)/shard_map/all_to_all | solution.py:114
  46.0 336.2 %all-to-all-start.3 = ((bf16[128,8,512]{0,2,1:T(8,128)(2,1)}), bf16[128,8,512]{0,2,1:T(8,128)(2,1)}, u32[]{:S(2)}, u32[]{:S(2)}) async-start(bf16[128,8,512]{0,2,1:T(8,128)(2,1)} %bitcast.30), calls=%async_computation.3 | async-start | bytes 2097152 | tf_op jit(solution)/shard_map/all_to_all | solution.py:115
  51.0 949.4 %all-gather.9.cloned.1.call-start = ((), (), s32[]{:S(2)}) async-start(), calls=%async_computation.6 | async-start | bytes 4456448 | tf_op jit(solution)/shard_map/all_gather | solution.py:155
  59.3 348.2 %copy-start = (f32[4,1024,128]{2,1,0:T(8,128)}, f32[4,1024,128]{2,1,0:T(8,128)S(1)}, u32[]{:S(2)}) copy-start(f32[4,1024,128]{2,1,0:T(8,128)S(1)} %copy.186) | copy-start | bytes 6291460
  391.7 2.4 copy-start.7
  391.7 2.9 copy-start.10
  398.3 9.2 copy-start.1
  473.6 4.7 copy-start.5
  474.5 525.9 %all-gather.11.cloned.1.call-start = ((), (), s32[]{:S(2)}) async-start(), calls=%async_computation.7 | async-start | bytes 4456448 | tf_op jit(solution)/shard_map/all_gather | solution.py:156
  508.5 1.9 copy-start.14
  508.5 1.9 copy-start.16
  841.3 2.1 copy-start.3
  858.4 242.7 %all-gather.13.cloned.1.call-start = ((), (), s32[]{:S(2)}) async-start(), calls=%async_computation.8 | async-start | bytes 4456448 | tf_op jit(solution)/shard_map/all_gather | solution.py:157
  923.1 19.9 %all-to-all-start.4 = ((bf16[128,8,512]{0,2,1:T(8,128)(2,1)}), bf16[128,8,512]{0,2,1:T(8,128)(2,1)}, u32[]{:S(2)}, u32[]{:S(2)}) async-start(bf16[128,8,512]{0,2,1:T(8,128)(2,1)} %bitcast.310), calls=%async_computation.4 | async-start | bytes 2097152 | tf_op jit(solution)/shard_map/all_to_all | solution.py:113
  927.8 173.4 %all-gather.15.cloned.1.call-start = ((), (), s32[]{:S(2)}) async-start(), calls=%async_computation.9 | async-start | bytes 4456448 | tf_op jit(solution)/shard_map/all_gather | solution.py:158
  977.7 4.1 copy-start.2
  981.8 3.5 copy-start.6
  985.3 3.6 copy-start.4
  992.5 4.1 copy-start.9
  (2 other events, 3.2 us)
Sparse Core Ops, SparseCore 0:
  474.6 52.8 all-gather.8
  858.5 52.6 all-gather.10
  920.9 52.5 all-gather.12
  1000.4 51.1 all-gather.14
where the time goes:
time: 1240 us; the launch traced here: 1230 us
  other arithmetic  652 us (53%)
  matrix products  316 us (25%)
  local copies, waits for them, and re-layouts  170 us (14%)
  waiting for transfers between devices  31.3 us (3%)
  starting transfers between devices  25 us (2%)
  blocking collectives  18.4 us (1%)
  between operations  13.9 us (1%)
    another operation x4, other arithmetic, span_parts(): jax.scipy.linalg.solve_triangular(system, right_side, lower=True, unit_di...  632 us
    dot_general x32, matrix products, step(): jnp.einsum('hck,hvk->hcv', effect_rows, carry, precision=highest)  53.5 us
    dot_general x32, matrix products, combine(): jnp.einsum('hij,hjk->hik', earlier[1], later[0], precision=highest)  45.7 us
    dot_general x32, matrix products, step(): jnp.einsum('hvj,hjk->hvk', carry, transit_step, precision=highest)  45.5 us
    dot_general x32, matrix products, combine(): jnp.einsum('hij,hjk->hik', earlier[0], later[0], precision=highest)  43.2 us
    unnamed x42, local copies, waits for them, and re-layouts  32.2 us
    dot_general x16, matrix products, take_upper(): jnp.einsum('hvj,hjk->hvk', state, every[2][source], precision=highest)  25 us
    dot_general x16, matrix products, take_lower(): jnp.einsum('hvj,hjk->hvk', state, every[0][step], precision=highest)  24.9 us
  transfers between devices with their start and end apart: 9, of which 4 were waited for; matrix products, arithmetic and copies ran while one was open for 76% of the time, Pallas kernels for 0%

commit v1 on v0

v1 whole, which is shorter than its diff:
```python
import functools

import jax
import jax.numpy as jnp
from jax import lax
from jax.experimental import pallas as pl
from jax.experimental.pallas import tpu as pltpu
from jax.sharding import Mesh, PartitionSpec as P

D = 128
C = 128
BASE = 32
EXTRA = 16
CUT = 128.0
F32 = jnp.float32
BF16 = jnp.bfloat16
GROUP = ("y", "z", "core")


def split(x):
    hi = x.astype(BF16)
    return hi, (x - hi.astype(F32)).astype(BF16)


def mm(a, b):
    return lax.dot_general(a, b, (((1,), (0,)), ((), ())), preferred_element_type=F32)


def mm_t(a, b):
    return lax.dot_general(a, b, (((1,), (1,)), ((), ())), preferred_element_type=F32)


def lhs3(pair):
    return jnp.concatenate([pair[0], pair[1], pair[0]], axis=1)


def rhs3(pair):
    return jnp.concatenate([pair[0], pair[0], pair[1]], axis=0)


def rhs3_t(pair):
    return jnp.concatenate([pair[0], pair[0], pair[1]], axis=1)


def dot3(a, b):
    return mm(lhs3(split(a)), rhs3(split(b)))


def dot_exact_rhs(a, b):
    return mm(jnp.concatenate(split(a), axis=1), jnp.concatenate([b, b], axis=0))


def iota(shape, dim):
    return lax.broadcasted_iota(jnp.int32, shape, dim)


def key_kernel(units, starts_ref, base_ref, kmsg_ref, a_hi, a_lo, w_ref, wg_ref, x_ref, y_ref, yt_ref, se_ref, rows_ref):
    step = pl.program_id(0)
    row, col = iota((C, C), 0), iota((C, C), 1)
    extra = kmsg_ref[:, C : C + EXTRA, :].astype(F32)
    beta = jnp.concatenate([extra[u, 0:1] for u in range(units)], axis=0)
    logd = jnp.concatenate([extra[u, 1:2] for u in range(units)], axis=0)
    level = mm(logd.astype(BF16), (row <= col).astype(BF16))
    begin = base_ref[0] + (step * units + iota((units, C), 0)) * C
    place = begin + iota((units, C), 1)
    cuts = jnp.zeros((units, C), F32)
    for n in range(starts_ref.shape[0]):
        at = starts_ref[n]
        cuts += jnp.where((begin < at) & (at <= place), 1.0, 0.0)
    level = level - CUT * cuts
    last = level[:, C - 1 : C]
    carried = jnp.exp(level)
    trail = jnp.exp(last - level)
    gate = jnp.exp(logd)
    inverse_gate = jnp.exp(-logd)
    eye = row == col
    keys = [kmsg_ref[u, :C, :] for u in range(units)]
    gram = [mm_t(k, k) for k in keys]
    norm = jnp.concatenate(
        [jnp.sum(jnp.where(eye, g, 0.0), axis=0, keepdims=True) for g in gram], axis=0
    )
    scale = 1.0 / jnp.sqrt(norm + 1e-6)
    columns = jnp.concatenate(
        [level, beta * scale, beta, carried * scale, inverse_gate], axis=0
    ).T

    def column(which, u):
        return columns[:, which * units + u : which * units + u + 1]

    same = (row // BASE) == (col // BASE)
    systems, compact = [], []
    for u in range(units):
        decay = jnp.exp(-jnp.abs(column(0, u) - level[u : u + 1]))
        weighted = decay * scale[u : u + 1]
        se_ref[u] = weighted
        system = jnp.where(row > col, gram[u] * weighted * column(1, u), 0.0)
        systems.append(system)
        inside = jnp.where(same, system, 0.0)
        compact.append(sum(inside[i * BASE : (i + 1) * BASE] for i in range(C // BASE)))
    lane = iota((BASE, C), 1)
    small_row = iota((BASE, C), 0)
    solved = [jnp.where(small_row == lane % BASE, 1.0, 0.0) for u in range(units)]
    first = (lane // BASE) * BASE
    for j in range(BASE - 1):
        top = (j // 8) * 8
        for u in range(units):
            factor = jnp.take_along_axis(compact[u][top:], first[top:] + j, axis=1)
            low = solved[u][top:] - factor * solved[u][j : j + 1]
            solved[u] = jnp.concatenate([solved[u][:top], low], axis=0) if top else low
    zero32 = jnp.zeros((BASE, C), F32)
    zero64 = jnp.zeros((2 * BASE, C), F32)
    full = [
        jnp.where(same, jnp.concatenate([solved[u]] * (C // BASE), axis=0), 0.0)
        for u in range(units)
    ]
    wide = iota((BASE, C), 1)
    part = []
    for u in range(units):
        left = jnp.concatenate(
            [
                jnp.where(wide < 32, systems[u][32:64], 0.0),
                jnp.where((wide >= 64) & (wide < 96), systems[u][96:128], 0.0),
            ],
            axis=0,
        )
        part.append(dot3(left, full[u]))
    for u in range(units):
        spread = jnp.concatenate([zero32, part[u][:32], zero32, part[u][32:]], axis=0)
        t = full[u]
        delta = dot3(jnp.concatenate([t[32:64], t[96:128]], axis=0), spread)
        full[u] = jnp.concatenate(
            [t[:32], t[32:64] - delta[:32], t[64:96], t[96:] - delta[32:]], axis=0
        )
    wide = iota((2 * BASE, C), 1)
    for u in range(units):
        part[u] = dot3(jnp.where(wide < 64, systems[u][64:], 0.0), full[u])
    for u in range(units):
        t = full[u]
        delta = dot3(t[64:], jnp.concatenate([zero64, part[u]], axis=0))
        full[u] = jnp.concatenate([t[:64], t[64:] - delta], axis=0)
    for u in range(units):
        one = slice(u, u + 1)
        y = full[u] * beta[one]
        y_ref[u] = y
        w = dot_exact_rhs(y * (scale[one] * carried[one]), keys[u])
        w_ref[u] = w
        wg_ref[u] = w * column(4, u)
        yt = full[u].T * column(2, u)
        yt_ref[u] = yt * inverse_gate[one]
        x = dot_exact_rhs(yt * (trail[one] * scale[one]), keys[u])
        x_ref[u] = x
        kt = keys[u].T
        back = jnp.concatenate(split(x * column(3, u)), axis=0)
        a = jnp.where(eye, carried[one, C - 1 : C], 0.0) - mm(jnp.concatenate([kt, kt], axis=1), back)
        hi, lo = split(a)
        a_hi[u] = hi
        a_lo[u] = lo
        rows_ref[u] = jnp.concatenate(
            [carried[one], trail[one], gate[one], jnp.zeros((5, C), F32)], axis=0
        )


def is_start(starts_ref, at):
    found = starts_ref[0] == at
    for n in range(1, starts_ref.shape[0]):
        found = found | (starts_ref[n] == at)
    return found


def scan_kernel(
    units, chunks, starts_ref, base_ref,
    af_hi, af_lo, vf_ref, x_ref, ab_hi, ab_lo, vb_ref, wg_ref, y_ref, yt_ref,
    zf_hi, zf_lo, zb_hi, zb_lo, uf_ref, ub_ref, total_ref, forward, backward,
):
    step = pl.program_id(0)

    @pl.when(step == 0)
    def _():
        start = jnp.concatenate(
            [jnp.zeros((D, D), F32), jnp.where(iota((D, D), 0) == iota((D, D), 1), 1.0, 0.0)],
            axis=0,
        )
        forward[...] = start
        backward[...] = start

    zf, zb = forward[...], backward[...]
    zero = jnp.zeros((D, D), F32)
    for u in range(units):
        n = step * units + u
        r = units - 1 - u
        m = chunks - 1 - n
        vt = vf_ref[u].T
        inject = mm(jnp.concatenate([vt, vt], axis=1), jnp.concatenate(split(x_ref[u]), axis=0))
        cut = is_start(starts_ref, base_ref[0] + n * C) & (n > 0)
        zf = zf * jnp.where(cut, 0.0, 1.0)
        pair = split(zf)
        zf_hi[u] = pair[0]
        zf_lo[u] = pair[1]
        zf = mm(lhs3(pair), rhs3((af_hi[u], af_lo[u]))) + jnp.concatenate([inject, zero], axis=0)
        vt = vb_ref[r].T
        inject = mm(jnp.concatenate([vt, vt], axis=1), jnp.concatenate(split(wg_ref[r]), axis=0))
        cut = is_start(starts_ref, base_ref[0] + (m + 1) * C) & (n > 0)
        zb = zb * jnp.where(cut, 0.0, 1.0)
        pair = split(zb)
        zb_hi[r] = pair[0]
        zb_lo[r] = pair[1]
        zb = mm_t(lhs3(pair), rhs3_t((ab_hi[r], ab_lo[r]))) + jnp.concatenate([inject, zero], axis=0)
        uf_ref[u] = dot_exact_rhs(y_ref[u], vf_ref[u])
        ub_ref[u] = dot_exact_rhs(yt_ref[u], vf_ref[u])
    forward[...] = zf
    backward[...] = zb
    total_ref[0] = zf[D:]
    total_ref[1] = zf[:D]
    total_ref[2] = zb[:D]


def query_kernel(units, q_ref, k_ref, se_ref, w_ref, x_ref, uf_ref, ub_ref, rows_ref, zf_hi, zf_lo, zb_hi, zb_lo, out_ref, f_ref):
    row, col = iota((C, C), 0), iota((C, C), 1)
    for u in range(units):
        q = q_ref[u]
        columns = rows_ref[u].T
        carried, trail, gate = columns[:, 0:1], columns[:, 1:2], columns[:, 2:3]
        scores = mm_t(q, k_ref[u]) * se_ref[u]
        lower = split(jnp.where(col <= row, scores, 0.0))
        upper = split(jnp.where(col > row, scores, 0.0))
        first = mm(lhs3(lower), rhs3(split(jnp.concatenate([uf_ref[u], w_ref[u]], axis=1))))
        second = mm(lhs3(upper), rhs3(split(jnp.concatenate([ub_ref[u], x_ref[u]], axis=1))))
        q = q.astype(F32)
        effect_f = carried * q - first[:, D:]
        effect_b = gate * (trail * q - second[:, D:])
        third = mm_t(lhs3(split(effect_f)), rhs3_t((zf_hi[u], zf_lo[u])))
        fourth = mm_t(lhs3(split(effect_b)), rhs3_t((zb_hi[u], zb_lo[u])))
        out_ref[u] = first[:, :D] + gate * second[:, :D] + third[:, :D] + fourth[:, :D]
        f_ref[u] = jnp.concatenate([third[:, D:], fourth[:, D:]], axis=1)


def final_kernel(units, starts_ref, base_ref, span, part_ref, f_ref, one_ref, two_ref, three_ref, mixed_ref, s_hi, s_lo):
    step = pl.program_id(0)

    @pl.when(step == 0)
    def _():
        mine = base_ref[0] // span
        arrived = {1: one_ref, 2: two_ref, 3: three_ref}
        sf = jnp.zeros((D, D), F32)
        for d in (3, 2, 1):
            cut = is_start(starts_ref, (mine - d) * span)
            moved = dot3(sf * jnp.where(cut, 0.0, 1.0), arrived[d][0]) + arrived[d][1]
            sf = jnp.where(d <= mine, moved, sf)
        sf = sf * jnp.where(is_start(starts_ref, mine * span), 0.0, 1.0)
        sb = jnp.zeros((D, D), F32)
        for d in (1, 2, 3):
            cut = is_start(starts_ref, (mine - d + 5) * span)
            moved = mm_t(
                lhs3(split(sb * jnp.where(cut, 0.0, 1.0))), rhs3_t(split(arrived[d][0]))
            ) + arrived[d][2]
            sb = jnp.where(d > mine, moved, sb)
        sb = sb * jnp.where(is_start(starts_ref, (mine + 1) * span), 0.0, 1.0)
        hi, lo = split(jnp.concatenate([sf, sb], axis=1))
        s_hi[...] = hi
        s_lo[...] = lo

    state = rhs3_t((s_hi[...], s_lo[...]))
    for u in range(units):
        mixed_ref[u] = (part_ref[u] + mm_t(lhs3(split(f_ref[u])), state)).astype(BF16)


def blocks(units, *tail, flip=None):
    if flip is None:
        return pl.BlockSpec((units,) + tail, lambda i: (i,) + (0,) * len(tail))
    return pl.BlockSpec((units,) + tail, lambda i: (flip - 1 - i,) + (0,) * len(tail))


SCALARS = [pl.BlockSpec(memory_space=pltpu.SMEM)] * 2


def params():
    return pltpu.CompilerParams(vmem_limit_bytes=48 * 1024 * 1024)


def cost(flops, moved):
    return pl.CostEstimate(flops=flops, bytes_accessed=moved, transcendentals=0)


def on_device(queries, keys, values, beta, log_decay, seg_lengths):
    own, width = queries.shape
    heads = width // D
    x = lax.axis_index("x")
    groups = lax.axis_size("x")
    chunks = heads
    span = chunks * C
    order = jnp.arange(seg_lengths.shape[0])
    starts = jnp.sum(jnp.where(order[None, :] < order[:, None], seg_lengths[None, :], 0), axis=1)
    starts = starts.astype(jnp.int32)
    base = (x * span).astype(jnp.int32).reshape(1)

    def by_head(array):
        return array.reshape(own, heads, D).transpose(1, 0, 2)

    def spread(array):
        return lax.all_to_all(array, GROUP, split_axis=0, concat_axis=0, tiled=True)

    extra = jnp.stack([beta.T, log_decay.T], axis=1)
    extra = jnp.concatenate([extra, jnp.zeros((heads, EXTRA - 2, C), BF16)], axis=1)
    kmsg = spread(jnp.concatenate([by_head(keys), extra], axis=1))
    v = spread(by_head(values))
    q = spread(by_head(queries))

    def out(*shape, dtype=F32):
        return jax.ShapeDtypeStruct((chunks,) + shape, dtype)

    units = 8
    a_hi, a_lo, w, wg, xx, y, yt, se, rows = pl.pallas_call(
        functools.partial(key_kernel, units),
        grid=(chunks // units,),
        in_specs=SCALARS + [blocks(units, C + EXTRA, D)],
        out_specs=[blocks(units, C, D)] * 8 + [blocks(units, 8, C)],
        out_shape=[out(C, D, dtype=BF16)] * 2 + [out(C, D)] * 6 + [out(8, C)],
        compiler_params=params(),
        cost_estimate=cost(20_000_000_000, 20_000_000),
        name="key_maps",
    )(starts, base, kmsg)
    n = chunks // units
    zf_hi, zf_lo, zb_hi, zb_lo, uf, ub, total = pl.pallas_call(
        functools.partial(scan_kernel, units, chunks),
        grid=(n,),
        in_specs=SCALARS
        + [blocks(units, C, D)] * 4
        + [blocks(units, C, D, flip=n)] * 4
        + [blocks(units, C, D)] * 2,
        out_specs=[blocks(units, 2 * C, D)] * 2
        + [blocks(units, 2 * C, D, flip=n)] * 2
        + [blocks(units, C, D)] * 2
        + [pl.BlockSpec((3, D, D), lambda i: (0, 0, 0))],
        out_shape=[out(2 * C, D, dtype=BF16)] * 4
        + [out(C, D)] * 2
        + [jax.ShapeDtypeStruct((3, D, D), F32)],
        scratch_shapes=[pltpu.VMEM((2 * D, D), F32)] * 2,
        compiler_params=params(),
        cost_estimate=cost(20_000_000_000, 20_000_000),
        name="scan",
    )(starts, base, a_hi, a_lo, v, xx, a_hi, a_lo, v, wg, y, yt)
    arrived = [
        lax.ppermute(total, "x", [(i, (i + d) % groups) for i in range(groups)]) for d in (1, 2, 3)
    ]
    part, f = pl.pallas_call(
        functools.partial(query_kernel, units),
        grid=(n,),
        in_specs=[blocks(units, C, D)] * 7
        + [blocks(units, 8, C)]
        + [blocks(units, 2 * C, D)] * 4,
        out_specs=[blocks(units, C, D), blocks(units, C, 2 * D)],
        out_shape=[out(C, D), out(C, 2 * D)],
        compiler_params=params(),
        cost_estimate=cost(20_000_000_000, 20_000_000),
        name="local_out",
    )(q, kmsg[:, :C, :], se, w, xx, uf, ub, rows, zf_hi, zf_lo, zb_hi, zb_lo)

    whole = pl.BlockSpec((3, D, D), lambda i: (0, 0, 0))

    def final(starts_ref, base_ref, *refs):
        final_kernel(units, starts_ref, base_ref, span, *refs)

    mixed = pl.pallas_call(
        final,
        grid=(n,),
        in_specs=SCALARS + [blocks(units, C, D), blocks(units, C, 2 * D)] + [whole] * 3,
        out_specs=blocks(units, C, D),
        out_shape=out(C, D, dtype=BF16),
        scratch_shapes=[pltpu.VMEM((D, 2 * D), BF16)] * 2,
        compiler_params=params(),
        cost_estimate=cost(2_000_000_000, 10_000_000),
        name="final",
    )(starts, base, part, f, *arrived)
    back = spread(mixed)
    return back.transpose(1, 0, 2).reshape(own, width)


def solution(mesh):
    fine = Mesh(mesh.devices.reshape(4, 4, 4, 2), ("x", "y", "z", "core"))
    rows = P(("x", "y", "z", "core"), None)
    return jax.shard_map(
        on_device,
        mesh=fine,
        in_specs=(rows,) * 5 + (P(),),
        out_specs=rows,
        check_vma=False,
    )
```

time: 1240 us -> 136 us (0.11)
  other arithmetic: 652 us -> 1.48 us
  matrix products: 316 us -> 0 us
  local copies, waits for them, and re-layouts: 170 us -> 16.6 us
  Pallas kernels: 0 us -> 52.7 us
  waiting for transfers between devices: 31.3 us -> 14.2 us
  between operations: 13.9 us -> 0.21 us
    another operation x9 -> x0, other arithmetic: 635 us -> none  [the longest x4 632 us: span_parts(): jax.scipy.linalg.solve_triangular(system, right_side, lower=True, unit_di...]
    dot_general x172 -> x0, matrix products: 309 us -> none  [the longest x32 53.5 us: step(): jnp.einsum('hck,hvk->hcv', effect_rows, carry, precision=highest)]
    rev x10 -> x0, local copies, waits for them, and re-layouts: 67.1 us -> none  [the longest x2 20.7 us: on_device(): query_heads[:, ::-1]]
    pallas_call x0 -> x4, Pallas kernels: none -> 52.7 us  [the longest x1 20.2 us: on_device(): pl.pallas_call(functools.partial(key_kernel, units), grid=(chunks // unit...]
    dynamic_slice x64 -> x0, local copies, waits for them, and re-layouts: 35.2 us -> none  [the longest x32 17.6 us: take_upper(): every[3][source]]
    unnamed x42 -> x29, local copies, waits for them, and re-layouts: 32.2 us -> 11.1 us
    all_to_all x5 -> x3, waiting for transfers between devices: 31.2 us -> 14.2 us  [spread(): return lax.all_to_all(array, GROUP, split_axis=0, concat_axis=0, tiled=True)]
    convert_element_type x10 -> x0, local copies, waits for them, and re-layouts: 16.2 us -> none  [the longest x6 15.4 us: by_head(): array.reshape(rows, heads, width).transpose(1, 0, 2).astype(jnp.float32)]
  transfers between devices with their start and end apart: 9 -> 6, of which waited for: 4 -> 1; matrix products, arithmetic and copies ran while one was open for 76% -> 3% of each run, Pallas kernels for 0% -> 35%
where the time goes in v1:
time: 136 us
  Pallas kernels  52.7 us (39%)
  starting transfers between devices  25.7 us (19%)
  blocking collectives  24.9 us (18%)
  local copies, waits for them, and re-layouts  16.6 us (12%)
  waiting for transfers between devices  14.2 us (10%)
  other arithmetic  1.48 us (1%)
    all_to_all x1, blocking collectives, spread(): return lax.all_to_all(array, GROUP, split_axis=0, concat_axis=0, tiled=True)  24.9 us
    all_to_all x3, starting transfers between devices, spread(): return lax.all_to_all(array, GROUP, split_axis=0, concat_axis=0, tiled=True)  20.9 us
    pallas_call x1, Pallas kernels, on_device(): pl.pallas_call(functools.partial(key_kernel, units), grid=(chunks // unit...  20.2 us
    pallas_call x1, Pallas kernels, on_device(): pl.pallas_call(functools.partial(query_kernel, units), grid=(n,), in_spec...  17.3 us
    all_to_all x3, waiting for transfers between devices, spread(): return lax.all_to_all(array, GROUP, split_axis=0, concat_axis=0, tiled=True)  14.2 us
    unnamed x29, local copies, waits for them, and re-layouts  11.1 us
    pallas_call x1, Pallas kernels, on_device(): pl.pallas_call(functools.partial(scan_kernel, units, chunks), grid=(n,),...  9.99 us
    pallas_call x1, Pallas kernels, on_device(): pl.pallas_call(final, grid=(n,), in_specs=SCALARS + [blocks(units, C, D),...  5.18 us
  transfers between devices with their start and end apart: 6, of which 1 were waited for; matrix products, arithmetic and copies ran while one was open for 3% of the time, Pallas kernels for 35%

profile of v1, /device:TPU:1, one launch (start us, length us, event | category | flops | bytes accessed | tf_op | source)
XLA Modules:
  0.0 135.8 jit_solution(16906988164645074279)
XLA Ops:
  0.0 1.6 %copy.19 = bf16[128,4096]{0,1:T(8,128)(2,1)S(1)} copy(bf16[128,4096]{1,0:T(8,128)(2,1)} %param.7) | data formatting | bytes 2097152 | tf_op args[1]
  2.5 1.4 %maximum_maximum_fusion = bf16[32,144,128]{2,1,0:T(8,128)(2,1)} fusion(bf16[32,1,128]{2,1,0:T(2,128)(2,1)S(1)} %copy.22, bf16[32,1,128]{2,1,0:T(2,128)(2,1)S(1)} %copy.21, bf16[32,128,128]{2,1,0:T(8,128)(2,1)S(1)} %bitcast.15, bf16[144]{0:T(256)(128)(2,1)S(1)} %pad.3.clone), kind=kLoop, calls=%fused_computation | loop fusion | flops 4718592 | bytes 2244896 | tf_op jit(solution)/shard_map/concatenate | solution.py:304
  3.8 9.6 %all-to-all-start.1 = ((bf16[32,144,128]{2,1,0:T(8,128)(2,1)}), bf16[32,144,128]{2,1,0:T(8,128)(2,1)S(1)}, u32[]{:S(2)}, u32[]{:S(2)}) async-start(bf16[32,144,128]{2,1,0:T(8,128)(2,1)} %maximum_maximum_fusion), calls=%async_computation.1 | async-start | bytes 2359296 | tf_op jit(solution)/shard_map/all_to_all | solution.py:300
  14.2 1.3 copy.24
  16.2 1.3 copy.18
  17.6 14.2 %all-to-all-done.1.kmsg_ref = bf16[32,144,128]{2,1,0:T(8,128)(2,1)S(1)} async-done(((bf16[32,144,128]{2,1,0:T(8,128)(2,1)}), bf16[32,144,128]{2,1,0:T(8,128)(2,1)S(1)}, u32[]{:S(2)}, u32[]{:S(2)}) %all-to-all-start.1) | async-done | bytes 1179680 | tf_op jit(solution)/shard_map/all_to_all | solution.py:300
  31.8 3.9 %all-to-all-start.2 = ((bf16[32,128,128]{2,1,0:T(8,128)(2,1)}), bf16[32,128,128]{2,1,0:T(8,128)(2,1)S(1)}, u32[]{:S(2)}, u32[]{:S(2)}) async-start(bf16[32,128,128]{2,1,0:T(8,128)(2,1)} %bitcast.10), calls=%async_computation.2 | async-start | bytes 2097152 | tf_op jit(solution)/shard_map/all_to_all | solution.py:300
  35.7 20.2 %key_maps.1 = (bf16[32,128,128]{2,1,0:T(8,128)(2,1)S(1)}, bf16[32,128,128]{2,1,0:T(8,128)(2,1)S(1)}, f32[32,128,128]{2,1,0:T(8,128)S(1)}, f32[32,128,128]{2,1,0:...) custom-call(s32[8]{0:T(128)S(1)} %select_reduce_fusion.starts_ref, ...), custom_call_target="tpu_custom_call" | custom-call | flops 20000000000 | bytes 20000000 | tf_op jit(solution)/shard_map/key_maps/pallas_call | solution.py:312
  55.9 1.4 %copy-done = f32[32,128,128]{2,1,0:T(8,128)} copy-done((f32[32,128,128]{2,1,0:T(8,128)}, f32[32,128,128]{2,1,0:T(8,128)S(1)}, u32[]{:S(2)}) %copy-start) | copy-done | bytes 2097176
  57.3 1.0 copy-done.2
  58.3 1.0 copy-done.4
  59.3 7.4 %all-to-all-start = ((bf16[32,128,128]{2,1,0:T(8,128)(2,1)}), bf16[32,128,128]{2,1,0:T(8,128)(2,1)S(1)}, u32[]{:S(2)}, u32[]{:S(2)}) async-start(bf16[32,128,128]{2,1,0:T(8,128)(2,1)} %bitcast.16), calls=%async_computation | async-start | bytes 2097152 | tf_op jit(solution)/shard_map/all_to_all | solution.py:300
  66.7 1.2 copy-done.3
  67.9 1.2 copy-done.5
  69.2 10.0 %scan.1 = (bf16[32,256,128]{2,1,0:T(8,128)(2,1)S(1)}, bf16[32,256,128]{2,1,0:T(8,128)(2,1)}, bf16[32,256,128]{2,1,0:T(8,128)(2,1)}, bf16[32,256,128]{2,1,0:T(8,1...) custom-call(s32[8]{0:T(128)S(1)} %select_reduce_fusion.starts_ref, ...), custom_call_target="tpu_custom_call" | custom-call | flops 20000000000 | bytes 20000000 | tf_op jit(solution)/shard_map/scan/pallas_call | solution.py:323
  79.2 1.3 copy-done.1
  80.5 1.2 collective-permute-start
  81.7 2.5 %collective-permute-start.1 = (f32[3,128,128]{2,1,0:T(8,128)}, f32[3,128,128]{2,1,0:T(8,128)}, u32[]{:S(2)}, u32[]{:S(2)}) collective-permute-start(f32[3,128,128]{2,1,0:T(8,128)} %get-tuple-element.40), channel_id=1, source_target_pairs={{0,64},{32,96},{64,0},{96,32},{1,65},{33,97},{65,1},{97,33},{2,66}... | collective-permute-start | bytes 589832 | tf_op jit(solution)/shard_map/ppermute | solution.py:343
  84.1 1.1 collective-permute-start.2
  85.4 0.9 copy-done.7
  86.3 17.3 %local_out.1 = (f32[32,128,128]{2,1,0:T(8,128)S(1)}, f32[32,128,256]{2,1,0:T(8,128)}) custom-call(bf16[32,128,128]{2,1,0:T(8,128)(2,1)S(1)} %all-to-all-done.q_ref, bf16[32,128,128]{2,1,0:T(8,128)(2,1)S(1)} %slice.4.k_ref, f32[32,128,128]{2,1,0:T(8,128)} %get-tuple-element.23.se_ref, f32[32,128,128]{2,1,0:T(8,128)} %copy-done, ...), custom_call_target="tpu_custom_call" | custom-call | flops 20000000000 | bytes 20000000 | tf_op jit(solution)/shard_map/local_out/pallas_call | solution.py:345
  103.7 5.2 %final.1 = bf16[32,128,128]{2,1,0:T(8,128)(2,1)S(1)} custom-call(s32[8]{0:T(128)S(1)} %select_reduce_fusion.starts_ref, s32[1]{0:T(128)} %bitcast.base_ref, f32[32,128,128]{2,1,0:T(8,128)S(1)} %get-tuple-element.38.refs_0_, f32[32,128,256]{2,1,0:T(8,128)} %get-tuple-element.39.refs_1_, f32[3,128,128]{2,1,0:T(8,128)S(1)} %collective-permute-done.refs_2_, ...), custom_call_target="tpu_custom_call" | custom-call | flops 2000000000 | bytes 10000000 | tf_op jit(solution)/shard_map/final/pallas_call | solution.py:363
  108.9 24.9 %all_to_all.20 = bf16[32,128,128]{2,1,0:T(8,128)(2,1)S(1)} all-to-all(bf16[32,128,128]{2,1,0:T(8,128)(2,1)S(1)} %final.1), channel_id=1, replica_groups=mesh['x'=4,'y'=4,'z'=4,'core'=2] {'y','z','core'}, dimensions={0} | all-to-all | bytes 2097152 | tf_op jit(solution)/shard_map/all_to_all | solution.py:300
  134.5 1.3 copy.26
  (34 shorter events, 3.1 us)
Async XLA Ops:
  0.0 2.3 %copy-start.10 = (bf16[128,32]{0,1:T(8,128)(2,1)S(1)}, bf16[128,32]{0,1:T(8,128)(2,1)}, u32[]{:S(2)}) copy-start(bf16[128,32]{0,1:T(8,128)(2,1)} %param.9) | copy-start | bytes 24580
  0.0 2.4 %copy-start.11 = (bf16[128,32]{0,1:T(8,128)(2,1)S(1)}, bf16[128,32]{0,1:T(8,128)(2,1)}, u32[]{:S(2)}) copy-start(bf16[128,32]{0,1:T(8,128)(2,1)} %param.10) | copy-start | bytes 24580
  2.5 11.0 %copy-start.8 = (bf16[128,4096]{1,0:T(8,128)(2,1)S(1)}, bf16[128,4096]{1,0:T(8,128)(2,1)}, u32[]{:S(2)}) copy-start(bf16[128,4096]{1,0:T(8,128)(2,1)} %param.8) | copy-start | bytes 3145732
  3.8 28.0 %all-to-all-start.1 = ((bf16[32,144,128]{2,1,0:T(8,128)(2,1)}), bf16[32,144,128]{2,1,0:T(8,128)(2,1)S(1)}, u32[]{:S(2)}, u32[]{:S(2)}) async-start(bf16[32,144,128]{2,1,0:T(8,128)(2,1)} %maximum_maximum_fusion), calls=%async_computation.1 | async-start | bytes 2359296 | tf_op jit(solution)/shard_map/all_to_all | solution.py:300
  14.2 1.4 copy-start.9
  15.5 2.0 %copy-start.12 = (s32[8]{0:T(128)S(1)}, s32[8]{0:T(128)}, u32[]{:S(2)}) copy-start(s32[8]{0:T(128)} %param.11) | copy-start | bytes 100
  31.8 27.5 %all-to-all-start.2 = ((bf16[32,128,128]{2,1,0:T(8,128)(2,1)}), bf16[32,128,128]{2,1,0:T(8,128)(2,1)S(1)}, u32[]{:S(2)}, u32[]{:S(2)}) async-start(bf16[32,128,128]{2,1,0:T(8,128)(2,1)} %bitcast.10), calls=%async_computation.2 | async-start | bytes 2097152 | tf_op jit(solution)/shard_map/all_to_all | solution.py:300
  55.9 1.4 %copy-start = (f32[32,128,128]{2,1,0:T(8,128)}, f32[32,128,128]{2,1,0:T(8,128)S(1)}, u32[]{:S(2)}) copy-start(f32[32,128,128]{2,1,0:T(8,128)S(1)} %get-tuple-element.24.w_ref) | copy-start | bytes 6291460
  57.3 1.0 copy-start.2
  58.3 1.0 copy-start.4
  59.3 19.9 %copy-start.6 = (f32[32,8,128]{2,1,0:T(8,128)}, f32[32,8,128]{2,1,0:T(8,128)S(1)}, u32[]{:S(2)}) copy-start(f32[32,8,128]{2,1,0:T(8,128)S(1)} %get-tuple-element.33.rows_ref) | copy-start | bytes 393220
  59.3 26.1 %all-to-all-start = ((bf16[32,128,128]{2,1,0:T(8,128)(2,1)}), bf16[32,128,128]{2,1,0:T(8,128)(2,1)S(1)}, u32[]{:S(2)}, u32[]{:S(2)}) async-start(bf16[32,128,128]{2,1,0:T(8,128)(2,1)} %bitcast.16), calls=%async_computation | async-start | bytes 2097152 | tf_op jit(solution)/shard_map/all_to_all | solution.py:300
  66.7 1.2 copy-start.3
  67.9 1.2 copy-start.5
  79.1 1.3 copy-start.1
  80.5 23.2 %collective-permute-start = (f32[3,128,128]{2,1,0:T(8,128)}, f32[3,128,128]{2,1,0:T(8,128)S(1)}, u32[]{:S(2)}, u32[]{:S(2)}) collective-permute-start(f32[3,128,128]{2,1,0:T(8,128)} %get-tuple-element.40), channel_id=1, source_target_pairs={{0,32},{32,64},{64,96},{96,0},{1,33},{33,65},{65,97},{97,1},{2,34}... | collective-permute-start | bytes 589832 | tf_op jit(solution)/shard_map/ppermute | solution.py:343
  81.7 22.0 %collective-permute-start.1 = (f32[3,128,128]{2,1,0:T(8,128)}, f32[3,128,128]{2,1,0:T(8,128)}, u32[]{:S(2)}, u32[]{:S(2)}) collective-permute-start(f32[3,128,128]{2,1,0:T(8,128)} %get-tuple-element.40), channel_id=1, source_target_pairs={{0,64},{32,96},{64,0},{96,32},{1,65},{33,97},{65,1},{97,33},{2,66}... | collective-permute-start | bytes 589832 | tf_op jit(solution)/shard_map/ppermute | solution.py:343
  84.1 19.5 %collective-permute-start.2 = (f32[3,128,128]{2,1,0:T(8,128)}, f32[3,128,128]{2,1,0:T(8,128)}, u32[]{:S(2)}, u32[]{:S(2)}) collective-permute-start(f32[3,128,128]{2,1,0:T(8,128)} %get-tuple-element.40), channel_id=1, source_target_pairs={{0,96},{32,0},{64,32},{96,64},{1,97},{33,1},{65,33},{97,65},{2,98}... | collective-permute-start | bytes 589832 | tf_op jit(solution)/shard_map/ppermute | solution.py:343
  85.4 0.9 copy-start.7

commit v2 on v1

v2 whole, which is shorter than its diff:
```python
import functools

import jax
import jax.numpy as jnp
from jax import lax
from jax.experimental import pallas as pl
from jax.experimental.pallas import tpu as pltpu
from jax.sharding import Mesh, PartitionSpec as P

D = 128
C = 128
BASE = 32
EXTRA = 16
CUT = 128.0
VMEM_MIB = 50
F32 = jnp.float32
BF16 = jnp.bfloat16
GROUP = ("y", "z", "core")


def split(x):
    hi = x.astype(BF16)
    return hi, (x - hi.astype(F32)).astype(BF16)


def mm(a, b):
    return lax.dot_general(a, b, (((1,), (0,)), ((), ())), preferred_element_type=F32)


def lhs3(pair):
    return jnp.concatenate([pair[0], pair[1], pair[0]], axis=1)


def rhs3(pair):
    return jnp.concatenate([pair[0], pair[0], pair[1]], axis=0)


def dot3(a, b):
    return mm(lhs3(split(a)), rhs3(split(b)))


def beside(x):
    return jnp.concatenate(split(x), axis=1)


def below(x):
    return jnp.concatenate(split(x), axis=0)


def twice(b, axis):
    return jnp.concatenate([b, b], axis=axis)


def widen(ab):
    return jnp.concatenate([ab, ab[:, : ab.shape[1] // 2]], axis=1)


def halves(ab):
    return ab[:, : ab.shape[1] // 2], ab[:, ab.shape[1] // 2 :]


def deepen(hi, lo):
    return jnp.concatenate([hi, hi, lo], axis=0)


def iota(shape, dim):
    return lax.broadcasted_iota(jnp.int32, shape, dim)


def key_kernel(units, starts_ref, base_ref, kmsg_ref, maps_ref, kt_ref, rows_ref):
    step = pl.program_id(0)
    row, col = iota((C, C), 0), iota((C, C), 1)
    extra = kmsg_ref[:, C : C + EXTRA, :].astype(F32)
    beta = jnp.concatenate([extra[u, 0:1] for u in range(units)], axis=0)
    logd = jnp.concatenate([extra[u, 1:2] for u in range(units)], axis=0)
    level = mm(logd.astype(BF16), (row <= col).astype(BF16))
    begin = base_ref[0] + (step * units + iota((units, C), 0)) * C
    place = begin + iota((units, C), 1)
    cuts = jnp.zeros((units, C), F32)
    for n in range(starts_ref.shape[0]):
        at = starts_ref[n]
        cuts += jnp.where((begin < at) & (at <= place), 1.0, 0.0)
    level = level - CUT * cuts
    last = level[:, C - 1 : C]
    carried = jnp.exp(level)
    trail = jnp.exp(last - level)
    gate = jnp.exp(logd)
    inverse_gate = jnp.exp(-logd)
    eye = row == col
    keys = [kmsg_ref[u, :C, :] for u in range(units)]
    turned = [k.T for k in keys]
    gram = [mm(keys[u], turned[u]) for u in range(units)]
    norm = jnp.concatenate(
        [jnp.sum(jnp.where(eye, g, 0.0), axis=0, keepdims=True) for g in gram], axis=0
    )
    scale = 1.0 / jnp.sqrt(norm + 1e-6)
    columns = jnp.concatenate(
        [level, beta * scale, beta, carried * scale, trail * scale], axis=0
    ).T

    def column(which, u):
        return columns[:, which * units + u : which * units + u + 1]

    same = (row // BASE) == (col // BASE)
    systems, compact = [], []
    for u in range(units):
        decay = jnp.exp(-jnp.abs(column(0, u) - level[u : u + 1]))
        weighted = decay * scale[u : u + 1]
        maps_ref[u, 8] = beside(weighted)
        system = jnp.where(row > col, gram[u] * weighted * column(1, u), 0.0)
        systems.append(system)
        inside = jnp.where(same, system, 0.0)
        compact.append(sum(inside[i * BASE : (i + 1) * BASE] for i in range(C // BASE)))
    lane = iota((BASE, C), 1)
    small_row = iota((BASE, C), 0)
    solved = [jnp.where(small_row == lane % BASE, 1.0, 0.0) for u in range(units)]
    first = (lane // BASE) * BASE
    for j in range(BASE - 1):
        top = (j // 8) * 8
        for u in range(units):
            factor = jnp.take_along_axis(compact[u][top:], first[top:] + j, axis=1)
            low = solved[u][top:] - factor * solved[u][j : j + 1]
            solved[u] = jnp.concatenate([solved[u][:top], low], axis=0) if top else low
    zero32 = jnp.zeros((BASE, C), F32)
    zero64 = jnp.zeros((2 * BASE, C), F32)
    full = [
        jnp.where(same, jnp.concatenate([solved[u]] * (C // BASE), axis=0), 0.0)
        for u in range(units)
    ]
    wide = iota((BASE, C), 1)
    part = []
    for u in range(units):
        left = jnp.concatenate(
            [
                jnp.where(wide < 32, systems[u][32:64], 0.0),
                jnp.where((wide >= 64) & (wide < 96), systems[u][96:128], 0.0),
            ],
            axis=0,
        )
        part.append(dot3(left, full[u]))
    for u in range(units):
        spread = jnp.concatenate([zero32, part[u][:32], zero32, part[u][32:]], axis=0)
        t = full[u]
        delta = dot3(jnp.concatenate([t[32:64], t[96:128]], axis=0), spread)
        full[u] = jnp.concatenate(
            [t[:32], t[32:64] - delta[:32], t[64:96], t[96:] - delta[32:]], axis=0
        )
    wide = iota((2 * BASE, C), 1)
    for u in range(units):
        part[u] = dot3(jnp.where(wide < 64, systems[u][64:], 0.0), full[u])
    for u in range(units):
        t = full[u]
        delta = dot3(t[64:], jnp.concatenate([zero64, part[u]], axis=0))
        full[u] = jnp.concatenate([t[:64], t[64:] - delta], axis=0)
    both = [None] * units
    for u in range(units):
        one = slice(u, u + 1)
        kt_ref[u] = turned[u]
        y = full[u] * beta[one]
        yt = full[u].T * column(2, u)
        maps_ref[u, 2] = beside(y)
        maps_ref[u, 5] = beside(yt * inverse_gate[one])
        right = jnp.concatenate([y * column(4, u), yt * column(3, u)], axis=1)
        both[u] = mm(twice(turned[u], 1), below(right))
    rests = [None] * units
    for u in range(units):
        one = slice(u, u + 1)
        xt, wt = both[u][:, :C], both[u][:, C:]
        rests[u] = mm(beside(xt * (carried[one] * scale[one])), twice(keys[u], 0))
        maps_ref[u, 1] = beside(xt)
        maps_ref[u, 4] = beside(wt * inverse_gate[one])
        maps_ref[u, 6] = beside(wt.T)
        maps_ref[u, 7] = beside(xt.T)
        rows_ref[u] = jnp.concatenate(
            [carried[one], trail[one], gate[one], jnp.zeros((5, C), F32)], axis=0
        )
    for u in range(units):
        at = jnp.where(eye, carried[u : u + 1, C - 1 : C], 0.0) - rests[u]
        maps_ref[u, 0] = beside(at)
        maps_ref[u, 3] = beside(at.T)


def is_start(starts_ref, at):
    found = starts_ref[0] == at
    for n in range(1, starts_ref.shape[0]):
        found = found | (starts_ref[n] == at)
    return found


def keep(cut):
    return jnp.where(cut, 0.0, 1.0)


def scan_kernel(
    units, chunks, starts_ref, base_ref, ff_ref, vf_ref, bb_ref, vb_ref,
    zf_ref, zb_ref, total_ref, forward, backward,
):
    step = pl.program_id(0)

    @pl.when(step == 0)
    def _():
        eye = jnp.where(iota((D, D), 0) == iota((D, D), 1), 1.0, 0.0)
        start = jnp.concatenate([jnp.zeros((D, D), F32), eye], axis=1)
        forward[...] = start
        backward[...] = start

    zero = jnp.zeros((D, D), F32)

    def prepare(maps_ref, v_ref, z_ref, u):
        v2 = twice(v_ref[u], 0)
        z_ref[u, 2] = beside(mm(maps_ref[u, 2], v2))
        return mm(maps_ref[u, 1], v2)

    def advance(z, cut, inject, maps_ref, z_ref, u):
        hi, lo = split(z * keep(cut))
        z_ref[u, 0] = hi
        z_ref[u, 1] = lo
        moved = mm(widen(maps_ref[u, 0]), deepen(hi, lo))
        return moved + jnp.concatenate([inject, zero], axis=1)

    inject_f = [prepare(ff_ref, vf_ref, zf_ref, u) for u in range(units)]
    inject_b = [prepare(bb_ref, vb_ref, zb_ref, u) for u in range(units)]
    zf, zb = forward[...], backward[...]
    for u in range(units):
        r = units - 1 - u
        n = step * units + u
        m = chunks - 1 - n
        cut_f = is_start(starts_ref, base_ref[0] + n * C) & (n > 0)
        cut_b = is_start(starts_ref, base_ref[0] + (m + 1) * C) & (n > 0)
        zf = advance(zf, cut_f, inject_f[u], ff_ref, zf_ref, u)
        zb = advance(zb, cut_b, inject_b[r], bb_ref, zb_ref, r)
    forward[...] = zf
    backward[...] = zb
    total_ref[0] = zf[:, D:]
    total_ref[1] = zf[:, :D]
    total_ref[2] = zb[:, :D]


def query_kernel(units, q_ref, kt_ref, maps_ref, rows_ref, zf_ref, zb_ref, f_ref):
    row, col = iota((C, C), 0), iota((C, C), 1)

    def pairs(one, two):
        one_hi, one_lo = halves(one)
        two_hi, two_lo = halves(two)
        return deepen(
            jnp.concatenate([one_hi, two_hi], axis=1), jnp.concatenate([one_lo, two_lo], axis=1)
        )

    every = range(units)
    columns = [rows_ref[u].T for u in every]
    scores = [mm(q_ref[u], kt_ref[u]) for u in every]
    first, second = [None] * units, [None] * units
    for u in every:
        se_hi, se_lo = halves(maps_ref[u, 2])
        score = scores[u] * (se_hi.astype(F32) + se_lo.astype(F32))
        lower = beside(jnp.where(col <= row, score, 0.0))
        upper = beside(jnp.where(col > row, score, 0.0))
        first[u] = mm(widen(lower), pairs(zf_ref[u, 2], maps_ref[u, 0]))
        second[u] = mm(widen(upper), pairs(zb_ref[u, 2], maps_ref[u, 1]))
    third, fourth = [None] * units, [None] * units
    for u in every:
        carried, trail, gate = (columns[u][:, i : i + 1] for i in range(3))
        q = q_ref[u].astype(F32)
        effect_f = carried * q - first[u][:, D:]
        effect_b = gate * (trail * q - second[u][:, D:])
        third[u] = mm(widen(beside(effect_f)), deepen(zf_ref[u, 0], zf_ref[u, 1]))
        fourth[u] = mm(widen(beside(effect_b)), deepen(zb_ref[u, 0], zb_ref[u, 1]))
    for u in every:
        gate = columns[u][:, 2:3]
        total = first[u][:, :D] + gate * second[u][:, :D] + third[u][:, :D] + fourth[u][:, :D]
        f_ref[u, 0] = beside(total)
        hi, lo = split(jnp.concatenate([third[u][:, D:], fourth[u][:, D:]], axis=1))
        f_ref[u, 1] = hi
        f_ref[u, 2] = lo


def final_kernel(units, span, starts_ref, base_ref, f_ref, one_ref, two_ref, three_ref, mixed_ref, state):
    step = pl.program_id(0)

    @pl.when(step == 0)
    def _():
        mine = base_ref[0] // span
        arrived = {1: one_ref, 2: two_ref, 3: three_ref}
        turned = {d: arrived[d][0].T for d in arrived}
        sf = jnp.zeros((D, D), F32)
        sb = jnp.zeros((D, D), F32)
        for d in (1, 2, 3):
            e = 4 - d
            cut = is_start(starts_ref, (mine - e) * span)
            moved = dot3(arrived[e][0], sf * keep(cut)) + arrived[e][1]
            sf = jnp.where(e <= mine, moved, sf)
            cut = is_start(starts_ref, (mine - d + 5) * span)
            moved = dot3(turned[d], sb * keep(cut)) + arrived[d][2]
            sb = jnp.where(d > mine, moved, sb)
        sf = sf * keep(is_start(starts_ref, mine * span))
        sb = sb * keep(is_start(starts_ref, (mine + 1) * span))
        state[...] = beside(jnp.concatenate([sf, sb], axis=0))

    def rows_of(which):
        return f_ref[:, which].reshape(units * C, 2 * D)

    wide = mm(rows_of(1), state[...])
    more = mm(rows_of(2), state[:, :D])
    hi, lo = halves(rows_of(0))
    total = (hi.astype(F32) + lo.astype(F32)) + (wide[:, :D] + wide[:, D:] + more)
    mixed_ref[...] = total.reshape(units, C, D).astype(BF16)


def pack_kernel(src_ref, dst_ref):
    for h in range(dst_ref.shape[0]):
        dst_ref[h] = src_ref[:, h * D : (h + 1) * D]


def pack_extra_kernel(src_ref, beta_ref, decay_ref, dst_ref):
    beta = beta_ref[...].astype(F32)
    decay = decay_ref[...].astype(F32)
    zero = jnp.zeros((EXTRA - 2, C), F32)
    for h in range(dst_ref.shape[0]):
        one = slice(h, h + 1)
        dst_ref[h, :C] = src_ref[:, h * D : (h + 1) * D]
        dst_ref[h, C:] = jnp.concatenate([beta[one], decay[one], zero], axis=0).astype(BF16)


def unpack_kernel(src_ref, dst_ref):
    for h in range(src_ref.shape[0]):
        dst_ref[:, h * D : (h + 1) * D] = src_ref[h]


def blocks(units, *tail, flip=None, group=0):
    back = (0,) * (len(tail) - 1)
    if flip is None:
        return pl.BlockSpec((units,) + tail, lambda i: (i, group) + back)
    return pl.BlockSpec((units,) + tail, lambda i: (flip - 1 - i, group) + back)


SCALARS = [pl.BlockSpec(memory_space=pltpu.SMEM)] * 2


def params():
    return pltpu.CompilerParams(vmem_limit_bytes=VMEM_MIB * 1024 * 1024)


def cost(flops, moved):
    return pl.CostEstimate(flops=flops, bytes_accessed=moved, transcendentals=0)


def pack(array, extra=None, units=16):
    own, width = array.shape
    heads = width // D
    rows = own + (EXTRA if extra is not None else 0)
    return pl.pallas_call(
        pack_kernel if extra is None else pack_extra_kernel,
        grid=(heads // units,),
        in_specs=[pl.BlockSpec((own, units * D), lambda i: (0, i))]
        + ([] if extra is None else [pl.BlockSpec((units, own), lambda i: (i, 0))] * 2),
        out_specs=blocks(units, rows, D),
        out_shape=jax.ShapeDtypeStruct((heads, rows, D), BF16),
        compiler_params=params(),
        cost_estimate=cost(0, 4_000_000),
        name="pack",
    )(*([array] if extra is None else [array, *extra]))


def unpack(array, units=16):
    heads, own, _ = array.shape
    return pl.pallas_call(
        unpack_kernel,
        grid=(heads // units,),
        in_specs=[blocks(units, own, D)],
        out_specs=pl.BlockSpec((own, units * D), lambda i: (0, i)),
        out_shape=jax.ShapeDtypeStruct((own, heads * D), BF16),
        compiler_params=params(),
        cost_estimate=cost(0, 4_000_000),
        name="unpack",
    )(array)


def triples(chunks, count=3):
    return jax.ShapeDtypeStruct((chunks, count, C, 2 * D), BF16)


def run_keys(starts, base, kmsg, units=8):
    chunks = kmsg.shape[0]
    return pl.pallas_call(
        functools.partial(key_kernel, units),
        grid=(chunks // units,),
        in_specs=SCALARS + [blocks(units, C + EXTRA, D)],
        out_specs=[blocks(units, 9, C, 2 * D), blocks(units, D, C), blocks(units, 8, C)],
        out_shape=[
            triples(chunks, 9),
            jax.ShapeDtypeStruct((chunks, D, C), BF16),
            jax.ShapeDtypeStruct((chunks, 8, C), F32),
        ],
        compiler_params=params(),
        cost_estimate=cost(20_000_000_000, 20_000_000),
        name="key_maps",
    )(starts, base, kmsg)


def run_scan(starts, base, v, maps, units=8):
    chunks = v.shape[0]
    n = chunks // units
    return pl.pallas_call(
        functools.partial(scan_kernel, units, chunks),
        grid=(n,),
        in_specs=SCALARS
        + [blocks(units, 3, C, 2 * D), blocks(units, C, D)]
        + [blocks(units, 3, C, 2 * D, flip=n, group=1), blocks(units, C, D, flip=n)],
        out_specs=[blocks(units, 3, C, 2 * D), blocks(units, 3, C, 2 * D, flip=n)]
        + [pl.BlockSpec((3, D, D), lambda i: (0, 0, 0))],
        out_shape=[triples(chunks)] * 2 + [jax.ShapeDtypeStruct((3, D, D), F32)],
        scratch_shapes=[pltpu.VMEM((D, 2 * D), F32)] * 2,
        compiler_params=params(),
        cost_estimate=cost(20_000_000_000, 20_000_000),
        name="scan",
    )(starts, base, maps, v, maps, v)


def run_queries(q, kt, maps, rows, zf, zb, units=16):
    chunks = q.shape[0]
    return pl.pallas_call(
        functools.partial(query_kernel, units),
        grid=(chunks // units,),
        in_specs=[blocks(units, C, D), blocks(units, D, C)]
        + [blocks(units, 3, C, 2 * D, group=2), blocks(units, 8, C)]
        + [blocks(units, 3, C, 2 * D)] * 2,
        out_specs=blocks(units, 3, C, 2 * D),
        out_shape=triples(chunks),
        compiler_params=params(),
        cost_estimate=cost(20_000_000_000, 20_000_000),
        name="local_out",
    )(q, kt, maps, rows, zf, zb)


def run_final(starts, base, f, arrived, units=16):
    chunks = f.shape[0]
    whole = pl.BlockSpec((3, D, D), lambda i: (0, 0, 0))
    return pl.pallas_call(
        functools.partial(final_kernel, units, chunks * C),
        grid=(chunks // units,),
        in_specs=SCALARS + [blocks(units, 3, C, 2 * D)] + [whole] * 3,
        out_specs=blocks(units, C, D),
        out_shape=jax.ShapeDtypeStruct((chunks, C, D), BF16),
        scratch_shapes=[pltpu.VMEM((2 * D, 2 * D), BF16)],
        compiler_params=params(),
        cost_estimate=cost(2_000_000_000, 10_000_000),
        name="final",
    )(starts, base, f, *arrived)


def spread(array):
    return lax.all_to_all(array, GROUP, split_axis=0, concat_axis=0, tiled=True)


def on_device(queries, keys, values, beta, log_decay, seg_lengths):
    heads = queries.shape[1] // D
    groups = lax.axis_size("x")
    order = jnp.arange(seg_lengths.shape[0])
    starts = jnp.sum(jnp.where(order[None, :] < order[:, None], seg_lengths[None, :], 0), axis=1)
    starts = starts.astype(jnp.int32)
    base = (lax.axis_index("x") * heads * C).astype(jnp.int32).reshape(1)
    kmsg = spread(pack(keys, (beta.T, log_decay.T)))
    v = spread(pack(values))
    q = spread(pack(queries))
    maps, kt, rows = run_keys(starts, base, kmsg)
    zf, zb, total = run_scan(starts, base, v, maps)
    arrived = [
        lax.ppermute(total, "x", [(i, (i + d) % groups) for i in range(groups)]) for d in (1, 2, 3)
    ]
    f = run_queries(q, kt, maps, rows, zf, zb)
    return unpack(spread(run_final(starts, base, f, arrived)))


def solution(mesh):
    fine = Mesh(mesh.devices.reshape(4, 4, 4, 2), ("x", "y", "z", "core"))
    rows = P(("x", "y", "z", "core"), None)
    return jax.shard_map(
        on_device,
        mesh=fine,
        in_specs=(rows,) * 5 + (P(),),
        out_specs=rows,
        check_vma=False,
    )
```

time: 136 us -> 118 us (0.87)
  local copies, waits for them, and re-layouts: 16.6 us -> 4.77 us
  Pallas kernels: 52.7 us -> 48.5 us
  starting transfers between devices: 25.7 us -> 23.7 us
  waiting for transfers between devices: 14.2 us -> 16.2 us
  other arithmetic: 1.48 us -> 0.11 us
    unnamed x29 -> x16, local copies, waits for them, and re-layouts: 11.1 us -> 4.77 us
    reshape x4 -> x0, local copies, waits for them, and re-layouts: 4.63 us -> none  [the longest x3 3.31 us: by_head(): return array.reshape(own, heads, D).transpose(1, 0, 2)]
    pallas_call x4 -> x8, Pallas kernels: 52.7 us -> 48.5 us  [the longest x1 16.1 us: run_keys(): pl.pallas_call(functools.partial(key_kernel, units), grid=(chunks // unit...]
    all_to_all x3, waiting for transfers between devices: 14.2 us -> 16.2 us  [spread(): return lax.all_to_all(array, GROUP, split_axis=0, concat_axis=0, tiled=True)]
    concatenate x1 -> x0, other arithmetic: 1.37 us -> none  [on_device(): kmsg = spread(jnp.concatenate([by_head(keys), extra], axis=1))]
  transfers between devices with their start and end apart: 6 -> 6, of which waited for: 1 -> 3; matrix products, arithmetic and copies ran while one was open for 3% -> 0% of each run, Pallas kernels for 35% -> 36%
where the time goes in v2:
time: 118 us
  Pallas kernels  48.5 us (41%)
  blocking collectives  24.3 us (21%)
  starting transfers between devices  23.7 us (20%)
  waiting for transfers between devices  16.2 us (14%)
  local copies, waits for them, and re-layouts  4.77 us (4%)
    all_to_all x1, blocking collectives, spread(): return lax.all_to_all(array, GROUP, split_axis=0, concat_axis=0, tiled=True)  24.3 us
    all_to_all x3, starting transfers between devices, spread(): return lax.all_to_all(array, GROUP, split_axis=0, concat_axis=0, tiled=True)  20.1 us
    all_to_all x3, waiting for transfers between devices, spread(): return lax.all_to_all(array, GROUP, split_axis=0, concat_axis=0, tiled=True)  16.2 us
    pallas_call x1, Pallas kernels, run_keys(): pl.pallas_call(functools.partial(key_kernel, units), grid=(chunks // unit...  16.1 us
    pallas_call x1, Pallas kernels, run_scan(): pl.pallas_call(functools.partial(scan_kernel, units, chunks), grid=(n,),...  12.7 us
    pallas_call x1, Pallas kernels, run_queries(): pl.pallas_call(functools.partial(query_kernel, units), grid=(chunks // un...  11.3 us
    unnamed x16, local copies, waits for them, and re-layouts  4.77 us
    pallas_call x1, Pallas kernels, run_final(): pl.pallas_call(functools.partial(final_kernel, units, chunks * C), grid=(...  3.95 us
  transfers between devices with their start and end apart: 6, of which 3 were waited for; matrix products, arithmetic and copies ran while one was open for 0% of the time, Pallas kernels for 36%

profile of v2, /device:TPU:1, one launch (start us, length us, event | category | flops | bytes accessed | tf_op | source)
XLA Modules:
  0.0 117.7 jit_solution(5249926630983648588)
XLA Ops:
  0.0 1.2 %copy-done = bf16[128,4096]{1,0:T(8,128)(2,1)S(1)} copy-done((bf16[128,4096]{1,0:T(8,128)(2,1)S(1)}, bf16[128,4096]{1,0:T(8,128)(2,1)}, u32[]{:S(2)}) %copy-start) | copy-done | bytes 1048600
  1.2 0.7 copy-done.3
  1.9 0.7 copy-done.4
  2.6 1.2 %pack.4 = bf16[32,144,128]{2,1,0:T(8,128)(2,1)} custom-call(bf16[128,4096]{1,0:T(8,128)(2,1)S(1)} %copy-done, bf16[32,128]{1,0:T(8,128)(2,1)S(1)} %bitcast.3, bf16[32,128]{1,0:T(8,128)(2,1)S(1)} %bitcast.4), custom_call_target="tpu_custom_call" | custom-call | bytes 4000000 | tf_op jit(solution)/shard_map/pack/pallas_call | solution.py:351
  3.9 9.6 %all-to-all-start.1 = ((bf16[32,144,128]{2,1,0:T(8,128)(2,1)}), bf16[32,144,128]{2,1,0:T(8,128)(2,1)S(1)}, u32[]{:S(2)}, u32[]{:S(2)}) async-start(bf16[32,144,128]{2,1,0:T(8,128)(2,1)} %pack.4), calls=%async_computation.1 | async-start | bytes 2359296 | tf_op jit(solution)/shard_map/all_to_all | solution.py:452
  13.5 1.2 %copy-done.1 = bf16[128,4096]{1,0:T(8,128)(2,1)S(1)} copy-done((bf16[128,4096]{1,0:T(8,128)(2,1)S(1)}, bf16[128,4096]{1,0:T(8,128)(2,1)}, u32[]{:S(2)}) %copy-start.1) | copy-done | bytes 1048600
  14.7 1.1 pack.3
  15.8 1.2 pack.5
  17.0 0.1 select_reduce_fusion.starts_ref
  17.1 14.7 %all-to-all-done.1.kmsg_ref = bf16[32,144,128]{2,1,0:T(8,128)(2,1)S(1)} async-done(((bf16[32,144,128]{2,1,0:T(8,128)(2,1)}), bf16[32,144,128]{2,1,0:T(8,128)(2,1)S(1)}, u32[]{:S(2)}, u32[]{:S(2)}) %all-to-all-start.1) | async-done | bytes 1179680 | tf_op jit(solution)/shard_map/all_to_all | solution.py:452
  31.8 3.9 %all-to-all-start.2 = ((bf16[32,128,128]{2,1,0:T(8,128)(2,1)}), bf16[32,128,128]{2,1,0:T(8,128)(2,1)S(1)}, u32[]{:S(2)}, u32[]{:S(2)}) async-start(bf16[32,128,128]{2,1,0:T(8,128)(2,1)} %pack.5), calls=%async_computation.2 | async-start | bytes 2097152 | tf_op jit(solution)/shard_map/all_to_all | solution.py:452
  35.7 16.1 %key_maps.1 = (bf16[32,9,128,256]{3,2,1,0:T(8,128)(2,1)}, bf16[32,128,128]{2,1,0:T(8,128)(2,1)S(1)}, f32[32,8,128]{2,1,0:T(8,128)S(1)}) custom-call(s32[8]{0:T(128)S(1)} %select_reduce_fusion.starts_ref, s32[1]{0:T(128)} %bitcast.base_ref, bf16[32,144,128]{2,1,0:T(8,128)(2,1)S(1)} %all-to-all-done.1.kmsg_ref), custom_call_target="tpu_custom_call" | custom-call | flops 20000000000 | bytes 20000000 | tf_op jit(solution)/shard_map/key_maps/pallas_call | solution.py:384
  51.8 0.9 all-to-all-done.2.vf_ref.vb_ref
  52.7 6.5 %all-to-all-start = ((bf16[32,128,128]{2,1,0:T(8,128)(2,1)}), bf16[32,128,128]{2,1,0:T(8,128)(2,1)S(1)}, u32[]{:S(2)}, u32[]{:S(2)}) async-start(bf16[32,128,128]{2,1,0:T(8,128)(2,1)} %pack.3), calls=%async_computation | async-start | bytes 2097152 | tf_op jit(solution)/shard_map/all_to_all | solution.py:452
  59.2 12.7 %scan.1 = (bf16[32,3,128,256]{3,2,1,0:T(8,128)(2,1)}, bf16[32,3,128,256]{3,2,1,0:T(8,128)(2,1)}, f32[3,128,128]{2,1,0:T(8,128)S(1)}) custom-call(s32[8]{0:T(128)S(1)} %select_reduce_fusion.starts_ref, s32[1]{0:T(128)} %bitcast.base_ref, bf16[32,9,128,256]{3,2,1,0:T(8,128)(2,1)} %get-tuple-element.12.ff_ref.bb_ref.maps_ref, ...), custom_call_target="tpu_custom_call" | custom-call | flops 20000000000 | bytes 20000000 | tf_op jit(solution)/shard_map/scan/pallas_call | solution.py:403
  71.9 2.5 %collective-permute-start.2 = (f32[3,128,128]{2,1,0:T(8,128)S(1)}, f32[3,128,128]{2,1,0:T(8,128)S(1)}, u32[]{:S(2)}, u32[]{:S(2)}) collective-permute-start(f32[3,128,128]{2,1,0:T(8,128)S(1)} %get-tuple-element.16), channel_id=1, source_target_pairs={{0,96},{32,0},{64,32},{96,64},{1,97},{33,1},{65,33},{97,65},{2,98}... | collective-permute-start | bytes 589832 | tf_op jit(solution)/shard_map/ppermute | solution.py:468
  74.4 0.5 collective-permute-start.1
  74.9 0.6 collective-permute-start
  75.5 0.7 all-to-all-done.q_ref
  76.1 0.9 copy-done.6
  77.0 11.3 %local_out.1.f_ref = bf16[32,3,128,256]{3,2,1,0:T(8,128)(2,1)} custom-call(bf16[32,128,128]{2,1,0:T(8,128)(2,1)S(1)} %all-to-all-done.q_ref, bf16[32,128,128]{2,1,0:T(8,128)(2,1)S(1)} %get-tuple-element.11.kt_ref, bf16[32,9,128,256]{3,2,1,0:T(8,128)(2,1)} %get-tuple-element.12.ff_ref.bb_ref.maps_ref, f32[32,8,128]{2,1,0:T(8,128)S(1)} %copy-done.6, ...), custom_call_target="tpu_custom_call" | custom-call | flops 20000000000 | bytes 20000000 | tf_op jit(solution)/shard_map/local_out/pallas_call | solution.py:421
  88.3 3.9 %final.1 = bf16[32,128,128]{2,1,0:T(8,128)(2,1)S(1)} custom-call(s32[8]{0:T(128)S(1)} %select_reduce_fusion.starts_ref, s32[1]{0:T(128)} %bitcast.base_ref, bf16[32,3,128,256]{3,2,1,0:T(8,128)(2,1)} %local_out.1.f_ref, f32[3,128,128]{2,1,0:T(8,128)S(1)} %collective-permute-done.one_ref, f32[3,128,128]{2,1,0:T(8,128)S(1)} %collective-permute-done.1.two_ref, ...), custom_call_target="tpu_custom_call" | custom-call | flops 2000000000 | bytes 10000000 | tf_op jit(solution)/shard_map/final/pallas_call | solution.py:438
  92.3 24.3 %all_to_all.20.src_ref = bf16[32,128,128]{2,1,0:T(8,128)(2,1)S(1)} all-to-all(bf16[32,128,128]{2,1,0:T(8,128)(2,1)S(1)} %final.1), channel_id=1, replica_groups=mesh['x'=4,'y'=4,'z'=4,'core'=2] {'y','z','core'}, dimensions={0} | all-to-all | bytes 2097152 | tf_op jit(solution)/shard_map/all_to_all | solution.py:452
  116.6 1.1 unpack.1
  (14 shorter events, 0.0 us)
Async XLA Ops:
  0.0 17.0 %copy-start.7 = (s32[8]{0:T(128)S(1)}, s32[8]{0:T(128)}, u32[]{:S(2)}) copy-start(s32[8]{0:T(128)} %param.11) | copy-start | bytes 100
  0.0 1.2 %copy-start = (bf16[128,4096]{1,0:T(8,128)(2,1)S(1)}, bf16[128,4096]{1,0:T(8,128)(2,1)}, u32[]{:S(2)}) copy-start(bf16[128,4096]{1,0:T(8,128)(2,1)} %src_ref.4) | copy-start | bytes 3145732
  1.2 0.7 copy-start.3
  1.9 0.7 copy-start.4
  2.6 13.2 %copy-start.2 = (bf16[128,4096]{1,0:T(8,128)(2,1)S(1)}, bf16[128,4096]{1,0:T(8,128)(2,1)}, u32[]{:S(2)}) copy-start(bf16[128,4096]{1,0:T(8,128)(2,1)} %src_ref.5) | copy-start | bytes 3145732
  3.9 28.0 %all-to-all-start.1 = ((bf16[32,144,128]{2,1,0:T(8,128)(2,1)}), bf16[32,144,128]{2,1,0:T(8,128)(2,1)S(1)}, u32[]{:S(2)}, u32[]{:S(2)}) async-start(bf16[32,144,128]{2,1,0:T(8,128)(2,1)} %pack.4), calls=%async_computation.1 | async-start | bytes 2359296 | tf_op jit(solution)/shard_map/all_to_all | solution.py:452
  13.5 1.2 %copy-start.1 = (bf16[128,4096]{1,0:T(8,128)(2,1)S(1)}, bf16[128,4096]{1,0:T(8,128)(2,1)}, u32[]{:S(2)}) copy-start(bf16[128,4096]{1,0:T(8,128)(2,1)} %src_ref.3) | copy-start | bytes 3145732
  31.8 20.9 %all-to-all-start.2 = ((bf16[32,128,128]{2,1,0:T(8,128)(2,1)}), bf16[32,128,128]{2,1,0:T(8,128)(2,1)S(1)}, u32[]{:S(2)}, u32[]{:S(2)}) async-start(bf16[32,128,128]{2,1,0:T(8,128)(2,1)} %pack.5), calls=%async_computation.2 | async-start | bytes 2097152 | tf_op jit(solution)/shard_map/all_to_all | solution.py:452
  51.8 7.4 %copy-start.5 = (f32[32,8,128]{2,1,0:T(8,128)}, f32[32,8,128]{2,1,0:T(8,128)S(1)}, u32[]{:S(2)}) copy-start(f32[32,8,128]{2,1,0:T(8,128)S(1)} %get-tuple-element.13.rows_ref) | copy-start | bytes 393220
  52.7 23.5 %all-to-all-start = ((bf16[32,128,128]{2,1,0:T(8,128)(2,1)}), bf16[32,128,128]{2,1,0:T(8,128)(2,1)S(1)}, u32[]{:S(2)}, u32[]{:S(2)}) async-start(bf16[32,128,128]{2,1,0:T(8,128)(2,1)} %pack.3), calls=%async_computation | async-start | bytes 2097152 | tf_op jit(solution)/shard_map/all_to_all | solution.py:452
  71.9 16.4 %collective-permute-start.2 = (f32[3,128,128]{2,1,0:T(8,128)S(1)}, f32[3,128,128]{2,1,0:T(8,128)S(1)}, u32[]{:S(2)}, u32[]{:S(2)}) collective-permute-start(f32[3,128,128]{2,1,0:T(8,128)S(1)} %get-tuple-element.16), channel_id=1, source_target_pairs={{0,96},{32,0},{64,32},{96,64},{1,97},{33,1},{65,33},{97,65},{2,98}... | collective-permute-start | bytes 589832 | tf_op jit(solution)/shard_map/ppermute | solution.py:468
  74.4 13.9 %collective-permute-start.1 = (f32[3,128,128]{2,1,0:T(8,128)S(1)}, f32[3,128,128]{2,1,0:T(8,128)S(1)}, u32[]{:S(2)}, u32[]{:S(2)}) collective-permute-start(f32[3,128,128]{2,1,0:T(8,128)S(1)} %get-tuple-element.16), channel_id=1, source_target_pairs={{0,64},{32,96},{64,0},{96,32},{1,65},{33,97},{65,1},{97,33},{2,66}... | collective-permute-start | bytes 589832 | tf_op jit(solution)/shard_map/ppermute | solution.py:468
  74.9 13.4 %collective-permute-start = (f32[3,128,128]{2,1,0:T(8,128)S(1)}, f32[3,128,128]{2,1,0:T(8,128)S(1)}, u32[]{:S(2)}, u32[]{:S(2)}) collective-permute-start(f32[3,128,128]{2,1,0:T(8,128)S(1)} %get-tuple-element.16), channel_id=1, source_target_pairs={{0,32},{32,64},{64,96},{96,0},{1,33},{33,65},{65,97},{97,1},{2,34}... | collective-permute-start | bytes 589832 | tf_op jit(solution)/shard_map/ppermute | solution.py:468
  76.1 0.9 copy-start.6

commit v3 on v2

--- a/solution.py
+++ b/solution.py
@@ -9,7 +9,7 @@
 
 D = 128
 C = 128
-BASE = 32
+BASE = 16
 EXTRA = 16
 CUT = 128.0
 VMEM_MIB = 50
@@ -121,37 +121,37 @@
             factor = jnp.take_along_axis(compact[u][top:], first[top:] + j, axis=1)
             low = solved[u][top:] - factor * solved[u][j : j + 1]
             solved[u] = jnp.concatenate([solved[u][:top], low], axis=0) if top else low
-    zero32 = jnp.zeros((BASE, C), F32)
-    zero64 = jnp.zeros((2 * BASE, C), F32)
     full = [
         jnp.where(same, jnp.concatenate([solved[u]] * (C // BASE), axis=0), 0.0)
         for u in range(units)
     ]
-    wide = iota((BASE, C), 1)
-    part = []
-    for u in range(units):
-        left = jnp.concatenate(
-            [
-                jnp.where(wide < 32, systems[u][32:64], 0.0),
-                jnp.where((wide >= 64) & (wide < 96), systems[u][96:128], 0.0),
-            ],
-            axis=0,
-        )
-        part.append(dot3(left, full[u]))
-    for u in range(units):
-        spread = jnp.concatenate([zero32, part[u][:32], zero32, part[u][32:]], axis=0)
-        t = full[u]
-        delta = dot3(jnp.concatenate([t[32:64], t[96:128]], axis=0), spread)
-        full[u] = jnp.concatenate(
-            [t[:32], t[32:64] - delta[:32], t[64:96], t[96:] - delta[32:]], axis=0
-        )
-    wide = iota((2 * BASE, C), 1)
-    for u in range(units):
-        part[u] = dot3(jnp.where(wide < 64, systems[u][64:], 0.0), full[u])
-    for u in range(units):
-        t = full[u]
-        delta = dot3(t[64:], jnp.concatenate([zero64, part[u]], axis=0))
-        full[u] = jnp.concatenate([t[:64], t[64:] - delta], axis=0)
+    half_row, half_col = iota((C // 2, C), 0), iota((C // 2, C), 1)
+    size = BASE
+    while size < C:
+        pieces = range(C // (2 * size))
+
+        def lower_rows(t):
+            return jnp.concatenate([t[(2 * i + 1) * size : (2 * i + 2) * size] for i in pieces], axis=0)
+
+        inside = (half_col // size) == 2 * (half_row // size)
+        zero = jnp.zeros((size, C), F32)
+        part = [
+            dot3(jnp.where(inside, lower_rows(systems[u]), 0.0), full[u]) for u in range(units)
+        ]
+        for u in range(units):
+            rows = [part[u][i * size : (i + 1) * size] for i in pieces]
+            spread = jnp.concatenate([block for r in rows for block in (zero, r)], axis=0)
+            part[u] = dot3(lower_rows(full[u]), spread)
+        for u in range(units):
+            t = full[u]
+            blocks_of = []
+            for i in pieces:
+                blocks_of.append(t[2 * i * size : (2 * i + 1) * size])
+                blocks_of.append(
+                    t[(2 * i + 1) * size : (2 * i + 2) * size] - part[u][i * size : (i + 1) * size]
+                )
+            full[u] = jnp.concatenate(blocks_of, axis=0)
+        size *= 2
     both = [None] * units
     for u in range(units):
         one = slice(u, u + 1)
@@ -207,28 +207,35 @@
     zero = jnp.zeros((D, D), F32)
 
     def prepare(maps_ref, v_ref, z_ref, u):
-        v2 = twice(v_ref[u], 0)
-        z_ref[u, 2] = beside(mm(maps_ref[u, 2], v2))
-        return mm(maps_ref[u, 1], v2)
-
-    def advance(z, cut, inject, maps_ref, z_ref, u):
-        hi, lo = split(z * keep(cut))
-        z_ref[u, 0] = hi
-        z_ref[u, 1] = lo
-        moved = mm(widen(maps_ref[u, 0]), deepen(hi, lo))
-        return moved + jnp.concatenate([inject, zero], axis=1)
+        both = mm(maps_ref[u, 1:3].reshape(2 * C, 2 * D), twice(v_ref[u], 0))
+        z_ref[u, 2] = beside(both[C:])
+        return both[:C]
+
+    def keep_state(z_ref, u, z):
+        pair = split(z)
+        z_ref[u, 0], z_ref[u, 1] = pair
+        return pair
+
+    def beyond(inject):
+        return jnp.concatenate([inject, zero], axis=1)
+
+    def keeps(u):
+        n = step * units + u
+        cut_f = is_start(starts_ref, base_ref[0] + n * C) & (n > 0)
+        cut_b = is_start(starts_ref, base_ref[0] + (chunks - n) * C) & (n > 0)
+        return keep(cut_f), keep(cut_b)
 
     inject_f = [prepare(ff_ref, vf_ref, zf_ref, u) for u in range(units)]
     inject_b = [prepare(bb_ref, vb_ref, zb_ref, u) for u in range(units)]
+    last = units - 1
     zf, zb = forward[...], backward[...]
     for u in range(units):
-        r = units - 1 - u
-        n = step * units + u
-        m = chunks - 1 - n
-        cut_f = is_start(starts_ref, base_ref[0] + n * C) & (n > 0)
-        cut_b = is_start(starts_ref, base_ref[0] + (m + 1) * C) & (n > 0)
-        zf = advance(zf, cut_f, inject_f[u], ff_ref, zf_ref, u)
-        zb = advance(zb, cut_b, inject_b[r], bb_ref, zb_ref, r)
+        r = last - u
+        kept_f, kept_b = keeps(u)
+        pair_f = keep_state(zf_ref, u, zf * kept_f)
+        pair_b = keep_state(zb_ref, r, zb * kept_b)
+        zf = mm(widen(ff_ref[u, 0]), deepen(*pair_f)) + beyond(inject_f[u])
+        zb = mm(widen(bb_ref[r, 0]), deepen(*pair_b)) + beyond(inject_b[r])
     forward[...] = zf
     backward[...] = zb
     total_ref[0] = zf[:, D:]
@@ -336,8 +343,8 @@
 SCALARS = [pl.BlockSpec(memory_space=pltpu.SMEM)] * 2
 
 
-def params():
-    return pltpu.CompilerParams(vmem_limit_bytes=VMEM_MIB * 1024 * 1024)
+def params(mib=VMEM_MIB):
+    return pltpu.CompilerParams(vmem_limit_bytes=mib * 1024 * 1024)
 
 
 def cost(flops, moved):
@@ -355,7 +362,7 @@
         + ([] if extra is None else [pl.BlockSpec((units, own), lambda i: (i, 0))] * 2),
         out_specs=blocks(units, rows, D),
         out_shape=jax.ShapeDtypeStruct((heads, rows, D), BF16),
-        compiler_params=params(),
+        compiler_params=params(60),
         cost_estimate=cost(0, 4_000_000),
         name="pack",
     )(*([array] if extra is None else [array, *extra]))
@@ -369,7 +376,7 @@
         in_specs=[blocks(units, own, D)],
         out_specs=pl.BlockSpec((own, units * D), lambda i: (0, i)),
         out_shape=jax.ShapeDtypeStruct((own, heads * D), BF16),
-        compiler_params=params(),
+        compiler_params=params(60),
         cost_estimate=cost(0, 4_000_000),
         name="unpack",
     )(array)
@@ -426,7 +433,7 @@
         + [blocks(units, 3, C, 2 * D)] * 2,
         out_specs=blocks(units, 3, C, 2 * D),
         out_shape=triples(chunks),
-        compiler_params=params(),
+        compiler_params=params(36),
         cost_estimate=cost(20_000_000_000, 20_000_000),
         name="local_out",
     )(q, kt, maps, rows, zf, zb)
@@ -442,7 +449,7 @@
         out_specs=blocks(units, C, D),
         out_shape=jax.ShapeDtypeStruct((chunks, C, D), BF16),
         scratch_shapes=[pltpu.VMEM((2 * D, 2 * D), BF16)],
-        compiler_params=params(),
+        compiler_params=params(36),
         cost_estimate=cost(2_000_000_000, 10_000_000),
         name="final",
     )(starts, base, f, *arrived)

time: 118 us -> 115 us (0.975)
  Pallas kernels: 48.5 us -> 46.9 us
  starting transfers between devices: 23.7 us -> 22.1 us
    pallas_call x3, Pallas kernels: 3.51 us -> 6.42 us  [pack(): pl.pallas_call(pack_kernel if extra is None else pack_extra_kernel, grid=...]
    pallas_call x1, Pallas kernels: 11.3 us -> 8.62 us  [run_queries(): pl.pallas_call(functools.partial(query_kernel, units), grid=(chunks // un...]
    all_to_all x3, starting transfers between devices: 20.1 us -> 18.5 us  [spread(): return lax.all_to_all(array, GROUP, split_axis=0, concat_axis=0, tiled=True)]
    pallas_call x1, Pallas kernels: 16.1 us -> 14.5 us  [run_keys(): pl.pallas_call(functools.partial(key_kernel, units), grid=(chunks // unit...]
    pallas_call x1, Pallas kernels: 3.95 us -> 2.57 us  [run_final(): pl.pallas_call(functools.partial(final_kernel, units, chunks * C), grid=(...]
    unnamed x16 -> x8, local copies, waits for them, and re-layouts: 4.77 us -> 3.7 us
  transfers between devices with their start and end apart: 6 -> 6, of which waited for: 3 -> 3; matrix products, arithmetic and copies ran while one was open for 0% -> 0% of each run, Pallas kernels for 36% -> 35%
where the time goes in v3:
time: 115 us; the launch traced here: 114 us
  Pallas kernels  46.9 us (41%)
  blocking collectives  24.4 us (21%)
  starting transfers between devices  22.1 us (19%)
  waiting for transfers between devices  17.1 us (15%)
  local copies, waits for them, and re-layouts  3.7 us (3%)
    all_to_all x1, blocking collectives, spread(): return lax.all_to_all(array, GROUP, split_axis=0, concat_axis=0, tiled=True)  24.4 us
    all_to_all x3, starting transfers between devices, spread(): return lax.all_to_all(array, GROUP, split_axis=0, concat_axis=0, tiled=True)  18.5 us
    all_to_all x3, waiting for transfers between devices, spread(): return lax.all_to_all(array, GROUP, split_axis=0, concat_axis=0, tiled=True)  17.1 us
    pallas_call x1, Pallas kernels, run_keys(): pl.pallas_call(functools.partial(key_kernel, units), grid=(chunks // unit...  14.5 us
    pallas_call x1, Pallas kernels, run_scan(): pl.pallas_call(functools.partial(scan_kernel, units, chunks), grid=(n,),...  12.6 us
    pallas_call x1, Pallas kernels, run_queries(): pl.pallas_call(functools.partial(query_kernel, units), grid=(chunks // un...  8.62 us
    pallas_call x3, Pallas kernels, pack(): pl.pallas_call(pack_kernel if extra is None else pack_extra_kernel, grid=...  6.42 us
    unnamed x8, local copies, waits for them, and re-layouts  3.7 us
  transfers between devices with their start and end apart: 6, of which 3 were waited for; matrix products, arithmetic and copies ran while one was open for 0% of the time, Pallas kernels for 35%

profile of v3, /device:TPU:1, one launch (start us, length us, event | category | flops | bytes accessed | tf_op | source)
XLA Modules:
  0.0 114.3 jit_solution(8022180060008437152)
XLA Ops:
  0.0 2.2 %pack.4 = bf16[32,144,128]{2,1,0:T(8,128)(2,1)} custom-call(bf16[128,4096]{1,0:T(8,128)(2,1)} %src_ref.4, bf16[32,128]{1,0:T(8,128)(2,1)} %bitcast.3, bf16[32,128]{1,0:T(8,128)(2,1)} %bitcast.4), custom_call_target="tpu_custom_call" | custom-call | bytes 4000000 | tf_op jit(solution)/shard_map/pack/pallas_call | solution.py:358
  2.2 9.6 %all-to-all-start.1 = ((bf16[32,144,128]{2,1,0:T(8,128)(2,1)}), bf16[32,144,128]{2,1,0:T(8,128)(2,1)S(1)}, u32[]{:S(2)}, u32[]{:S(2)}) async-start(bf16[32,144,128]{2,1,0:T(8,128)(2,1)} %pack.4), calls=%async_computation.1 | async-start | bytes 2359296 | tf_op jit(solution)/shard_map/all_to_all | solution.py:459
  11.8 2.1 %pack.3 = bf16[32,128,128]{2,1,0:T(8,128)(2,1)} custom-call(bf16[128,4096]{1,0:T(8,128)(2,1)} %src_ref.3), custom_call_target="tpu_custom_call" | custom-call | bytes 4000000 | tf_op jit(solution)/shard_map/pack/pallas_call | solution.py:358
  13.9 2.1 %pack.5 = bf16[32,128,128]{2,1,0:T(8,128)(2,1)} custom-call(bf16[128,4096]{1,0:T(8,128)(2,1)} %src_ref.5), custom_call_target="tpu_custom_call" | custom-call | bytes 4000000 | tf_op jit(solution)/shard_map/pack/pallas_call | solution.py:358
  16.0 0.1 select_reduce_fusion.starts_ref
  16.2 14.0 %all-to-all-done.1.kmsg_ref = bf16[32,144,128]{2,1,0:T(8,128)(2,1)S(1)} async-done(((bf16[32,144,128]{2,1,0:T(8,128)(2,1)}), bf16[32,144,128]{2,1,0:T(8,128)(2,1)S(1)}, u32[]{:S(2)}, u32[]{:S(2)}) %all-to-all-start.1) | async-done | bytes 1179680 | tf_op jit(solution)/shard_map/all_to_all | solution.py:459
  30.2 3.9 %all-to-all-start.2 = ((bf16[32,128,128]{2,1,0:T(8,128)(2,1)}), bf16[32,128,128]{2,1,0:T(8,128)(2,1)S(1)}, u32[]{:S(2)}, u32[]{:S(2)}) async-start(bf16[32,128,128]{2,1,0:T(8,128)(2,1)} %pack.5), calls=%async_computation.2 | async-start | bytes 2097152 | tf_op jit(solution)/shard_map/all_to_all | solution.py:459
  34.1 14.5 %key_maps.1 = (bf16[32,9,128,256]{3,2,1,0:T(8,128)(2,1)}, bf16[32,128,128]{2,1,0:T(8,128)(2,1)S(1)}, f32[32,8,128]{2,1,0:T(8,128)S(1)}) custom-call(s32[8]{0:T(128)S(1)} %select_reduce_fusion.starts_ref, s32[1]{0:T(128)} %bitcast.base_ref, bf16[32,144,128]{2,1,0:T(8,128)(2,1)S(1)} %all-to-all-done.1.kmsg_ref), custom_call_target="tpu_custom_call" | custom-call | flops 20000000000 | bytes 20000000 | tf_op jit(solution)/shard_map/key_maps/pallas_call | solution.py:391
  48.5 2.5 %all-to-all-done.2.vf_ref.vb_ref = bf16[32,128,128]{2,1,0:T(8,128)(2,1)S(1)} async-done(((bf16[32,128,128]{2,1,0:T(8,128)(2,1)}), bf16[32,128,128]{2,1,0:T(8,128)(2,1)S(1)}, u32[]{:S(2)}, u32[]{:S(2)}) %all-to-all-start.2) | async-done | bytes 1048608 | tf_op jit(solution)/shard_map/all_to_all | solution.py:459
  51.0 4.9 %all-to-all-start = ((bf16[32,128,128]{2,1,0:T(8,128)(2,1)}), bf16[32,128,128]{2,1,0:T(8,128)(2,1)S(1)}, u32[]{:S(2)}, u32[]{:S(2)}) async-start(bf16[32,128,128]{2,1,0:T(8,128)(2,1)} %pack.3), calls=%async_computation | async-start | bytes 2097152 | tf_op jit(solution)/shard_map/all_to_all | solution.py:459
  56.0 12.6 %scan.1 = (bf16[32,3,128,256]{3,2,1,0:T(8,128)(2,1)}, bf16[32,3,128,256]{3,2,1,0:T(8,128)(2,1)}, f32[3,128,128]{2,1,0:T(8,128)S(1)}) custom-call(s32[8]{0:T(128)S(1)} %select_reduce_fusion.starts_ref, s32[1]{0:T(128)} %bitcast.base_ref, bf16[32,9,128,256]{3,2,1,0:T(8,128)(2,1)} %get-tuple-element.12.ff_ref.bb_ref.maps_ref, ...), custom_call_target="tpu_custom_call" | custom-call | flops 20000000000 | bytes 20000000 | tf_op jit(solution)/shard_map/scan/pallas_call | solution.py:410
  68.6 2.5 %collective-permute-start.2 = (f32[3,128,128]{2,1,0:T(8,128)S(1)}, f32[3,128,128]{2,1,0:T(8,128)S(1)}, u32[]{:S(2)}, u32[]{:S(2)}) collective-permute-start(f32[3,128,128]{2,1,0:T(8,128)S(1)} %get-tuple-element.16), channel_id=1, source_target_pairs={{0,96},{32,0},{64,32},{96,64},{1,97},{33,1},{65,33},{97,65},{2,98}... | collective-permute-start | bytes 589832 | tf_op jit(solution)/shard_map/ppermute | solution.py:475
  71.1 0.5 collective-permute-start.1
  71.6 0.6 collective-permute-start
  72.2 0.6 all-to-all-done.q_ref
  72.9 2.8 %copy-done = bf16[32,3,128,256]{3,2,1,0:T(8,128)(2,1)S(1)} copy-done((bf16[32,3,128,256]{3,2,1,0:T(8,128)(2,1)S(1)}, bf16[32,3,128,256]{3,2,1,0:T(8,128)(2,1)}, u32[]{:S(2)}) %copy-start) | copy-done | bytes 6291480
  75.7 0.9 copy-done.2
  76.6 8.6 %local_out.1.f_ref = bf16[32,3,128,256]{3,2,1,0:T(8,128)(2,1)S(1)} custom-call(bf16[32,128,128]{2,1,0:T(8,128)(2,1)S(1)} %all-to-all-done.q_ref, bf16[32,128,128]{2,1,0:T(8,128)(2,1)S(1)} %get-tuple-element.11.kt_ref, bf16[32,9,128,256]{3,2,1,0:T(8,128)(2,1)} %get-tuple-element.12.ff_ref.bb_ref.maps_ref, f32[32,8,128]{2,1,0:T(8,128)S(1)} %copy-done.2, ...), custom_call_target="tpu_custom_call" | custom-call | flops 20000000000 | bytes 20000000 | tf_op jit(solution)/shard_map/local_out/pallas_call | solution.py:428
  85.2 0.0 collective-permute-done.2.three_ref
  85.2 0.0 collective-permute-done.1.two_ref
  85.2 0.0 collective-permute-done.one_ref
  85.2 2.6 %final.1 = bf16[32,128,128]{2,1,0:T(8,128)(2,1)S(1)} custom-call(s32[8]{0:T(128)S(1)} %select_reduce_fusion.starts_ref, s32[1]{0:T(128)} %bitcast.base_ref, bf16[32,3,128,256]{3,2,1,0:T(8,128)(2,1)S(1)} %local_out.1.f_ref, f32[3,128,128]{2,1,0:T(8,128)S(1)} %collective-permute-done.one_ref, f32[3,128,128]{2,1,0:T(8,128)S(1)} %collective-permute-done.1.two_ref, ...), custom_call_target="tpu_custom_call" | custom-call | flops 2000000000 | bytes 10000000 | tf_op jit(solution)/shard_map/final/pallas_call | solution.py:445
  87.8 24.4 %all_to_all.20.src_ref = bf16[32,128,128]{2,1,0:T(8,128)(2,1)} all-to-all(bf16[32,128,128]{2,1,0:T(8,128)(2,1)S(1)} %final.1), channel_id=1, replica_groups=mesh['x'=4,'y'=4,'z'=4,'core'=2] {'y','z','core'}, dimensions={0} | all-to-all | bytes 2097152 | tf_op jit(solution)/shard_map/all_to_all | solution.py:459
  112.2 2.1 %unpack.1 = bf16[128,4096]{1,0:T(8,128)(2,1)} custom-call(bf16[32,128,128]{2,1,0:T(8,128)(2,1)} %all_to_all.20.src_ref), custom_call_target="tpu_custom_call" | custom-call | bytes 4000000 | tf_op jit(solution)/shard_map/unpack/pallas_call | solution.py:373
  (6 shorter events, 0.0 us)
Async XLA Ops:
  0.0 16.0 %copy-start.3 = (s32[8]{0:T(128)S(1)}, s32[8]{0:T(128)}, u32[]{:S(2)}) copy-start(s32[8]{0:T(128)} %param.11) | copy-start | bytes 100
  2.2 28.0 %all-to-all-start.1 = ((bf16[32,144,128]{2,1,0:T(8,128)(2,1)}), bf16[32,144,128]{2,1,0:T(8,128)(2,1)S(1)}, u32[]{:S(2)}, u32[]{:S(2)}) async-start(bf16[32,144,128]{2,1,0:T(8,128)(2,1)} %pack.4), calls=%async_computation.1 | async-start | bytes 2359296 | tf_op jit(solution)/shard_map/all_to_all | solution.py:459
  30.2 20.8 %all-to-all-start.2 = ((bf16[32,128,128]{2,1,0:T(8,128)(2,1)}), bf16[32,128,128]{2,1,0:T(8,128)(2,1)S(1)}, u32[]{:S(2)}, u32[]{:S(2)}) async-start(bf16[32,128,128]{2,1,0:T(8,128)(2,1)} %pack.5), calls=%async_computation.2 | async-start | bytes 2097152 | tf_op jit(solution)/shard_map/all_to_all | solution.py:459
  48.5 7.4 %copy-start.1 = (f32[32,8,128]{2,1,0:T(8,128)}, f32[32,8,128]{2,1,0:T(8,128)S(1)}, u32[]{:S(2)}) copy-start(f32[32,8,128]{2,1,0:T(8,128)S(1)} %get-tuple-element.13.rows_ref) | copy-start | bytes 393220
  51.0 21.9 %all-to-all-start = ((bf16[32,128,128]{2,1,0:T(8,128)(2,1)}), bf16[32,128,128]{2,1,0:T(8,128)(2,1)S(1)}, u32[]{:S(2)}, u32[]{:S(2)}) async-start(bf16[32,128,128]{2,1,0:T(8,128)(2,1)} %pack.3), calls=%async_computation | async-start | bytes 2097152 | tf_op jit(solution)/shard_map/all_to_all | solution.py:459
  68.6 16.6 %collective-permute-start.2 = (f32[3,128,128]{2,1,0:T(8,128)S(1)}, f32[3,128,128]{2,1,0:T(8,128)S(1)}, u32[]{:S(2)}, u32[]{:S(2)}) collective-permute-start(f32[3,128,128]{2,1,0:T(8,128)S(1)} %get-tuple-element.16), channel_id=1, source_target_pairs={{0,96},{32,0},{64,32},{96,64},{1,97},{33,1},{65,33},{97,65},{2,98}... | collective-permute-start | bytes 589832 | tf_op jit(solution)/shard_map/ppermute | solution.py:475
  71.1 14.1 %collective-permute-start.1 = (f32[3,128,128]{2,1,0:T(8,128)S(1)}, f32[3,128,128]{2,1,0:T(8,128)S(1)}, u32[]{:S(2)}, u32[]{:S(2)}) collective-permute-start(f32[3,128,128]{2,1,0:T(8,128)S(1)} %get-tuple-element.16), channel_id=1, source_target_pairs={{0,64},{32,96},{64,0},{96,32},{1,65},{33,97},{65,1},{97,33},{2,66}... | collective-permute-start | bytes 589832 | tf_op jit(solution)/shard_map/ppermute | solution.py:475
  71.6 13.6 %collective-permute-start = (f32[3,128,128]{2,1,0:T(8,128)S(1)}, f32[3,128,128]{2,1,0:T(8,128)S(1)}, u32[]{:S(2)}, u32[]{:S(2)}) collective-permute-start(f32[3,128,128]{2,1,0:T(8,128)S(1)} %get-tuple-element.16), channel_id=1, source_target_pairs={{0,32},{32,64},{64,96},{96,0},{1,33},{33,65},{65,97},{97,1},{2,34}... | collective-permute-start | bytes 589832 | tf_op jit(solution)/shard_map/ppermute | solution.py:475
  72.9 2.8 %copy-start = (bf16[32,3,128,256]{3,2,1,0:T(8,128)(2,1)S(1)}, bf16[32,3,128,256]{3,2,1,0:T(8,128)(2,1)}, u32[]{:S(2)}) copy-start(bf16[32,3,128,256]{3,2,1,0:T(8,128)(2,1)} %get-tuple-element.14.zf_ref) | copy-start | bytes 18874372
  75.7 0.9 copy-start.2

commit v4 on v3

--- a/solution.py
+++ b/solution.py
@@ -67,7 +67,7 @@
     return lax.broadcasted_iota(jnp.int32, shape, dim)
 
 
-def key_kernel(units, starts_ref, base_ref, kmsg_ref, maps_ref, kt_ref, rows_ref):
+def key_kernel(units, starts_ref, base_ref, kmsg_ref, maps_ref):
     step = pl.program_id(0)
     row, col = iota((C, C), 0), iota((C, C), 1)
     extra = kmsg_ref[:, C : C + EXTRA, :].astype(F32)
@@ -155,7 +155,6 @@
     both = [None] * units
     for u in range(units):
         one = slice(u, u + 1)
-        kt_ref[u] = turned[u]
         y = full[u] * beta[one]
         yt = full[u].T * column(2, u)
         maps_ref[u, 2] = beside(y)
@@ -171,9 +170,10 @@
         maps_ref[u, 4] = beside(wt * inverse_gate[one])
         maps_ref[u, 6] = beside(wt.T)
         maps_ref[u, 7] = beside(xt.T)
-        rows_ref[u] = jnp.concatenate(
-            [carried[one], trail[one], gate[one], jnp.zeros((5, C), F32)], axis=0
-        )
+        rows = jnp.concatenate([carried[one], trail[one], gate[one], jnp.zeros((5, C), F32)], axis=0)
+        hi = rows.astype(BF16).astype(F32)
+        rows = jnp.concatenate([hi, rows - hi, jnp.zeros((C - 16, C), F32)], axis=0).astype(BF16)
+        maps_ref[u, 9] = jnp.concatenate([turned[u], rows], axis=1)
     for u in range(units):
         at = jnp.where(eye, carried[u : u + 1, C - 1 : C], 0.0) - rests[u]
         maps_ref[u, 0] = beside(at)
@@ -225,8 +225,14 @@
         cut_b = is_start(starts_ref, base_ref[0] + (chunks - n) * C) & (n > 0)
         return keep(cut_f), keep(cut_b)
 
-    inject_f = [prepare(ff_ref, vf_ref, zf_ref, u) for u in range(units)]
-    inject_b = [prepare(bb_ref, vb_ref, zb_ref, u) for u in range(units)]
+    inject_f, inject_b = {}, {}
+
+    def ready(u):
+        if u < units:
+            inject_f[u] = prepare(ff_ref, vf_ref, zf_ref, u)
+            inject_b[units - 1 - u] = prepare(bb_ref, vb_ref, zb_ref, units - 1 - u)
+
+    ready(0)
     last = units - 1
     zf, zb = forward[...], backward[...]
     for u in range(units):
@@ -234,8 +240,11 @@
         kept_f, kept_b = keeps(u)
         pair_f = keep_state(zf_ref, u, zf * kept_f)
         pair_b = keep_state(zb_ref, r, zb * kept_b)
-        zf = mm(widen(ff_ref[u, 0]), deepen(*pair_f)) + beyond(inject_f[u])
-        zb = mm(widen(bb_ref[r, 0]), deepen(*pair_b)) + beyond(inject_b[r])
+        zf = mm(widen(ff_ref[u, 0]), deepen(*pair_f))
+        zb = mm(widen(bb_ref[r, 0]), deepen(*pair_b))
+        ready(u + 1)
+        zf = zf + beyond(inject_f[u])
+        zb = zb + beyond(inject_b[r])
     forward[...] = zf
     backward[...] = zb
     total_ref[0] = zf[:, D:]
@@ -243,7 +252,7 @@
     total_ref[2] = zb[:, :D]
 
 
-def query_kernel(units, q_ref, kt_ref, maps_ref, rows_ref, zf_ref, zb_ref, f_ref):
+def query_kernel(units, q_ref, maps_ref, more_ref, zf_ref, zb_ref, f_ref):
     row, col = iota((C, C), 0), iota((C, C), 1)
 
     def pairs(one, two):
@@ -254,8 +263,9 @@
         )
 
     every = range(units)
-    columns = [rows_ref[u].T for u in every]
-    scores = [mm(q_ref[u], kt_ref[u]) for u in every]
+    rows = [more_ref[u, 0, :16, C:].astype(F32) for u in every]
+    columns = [(rows[u][:8] + rows[u][8:]).T for u in every]
+    scores = [mm(q_ref[u], more_ref[u, 0, :, :C]) for u in every]
     first, second = [None] * units, [None] * units
     for u in every:
         se_hi, se_lo = halves(maps_ref[u, 2])
@@ -376,7 +386,7 @@
         in_specs=[blocks(units, own, D)],
         out_specs=pl.BlockSpec((own, units * D), lambda i: (0, i)),
         out_shape=jax.ShapeDtypeStruct((own, heads * D), BF16),
-        compiler_params=params(60),
+        compiler_params=params(36),
         cost_estimate=cost(0, 4_000_000),
         name="unpack",
     )(array)
@@ -392,12 +402,8 @@
         functools.partial(key_kernel, units),
         grid=(chunks // units,),
         in_specs=SCALARS + [blocks(units, C + EXTRA, D)],
-        out_specs=[blocks(units, 9, C, 2 * D), blocks(units, D, C), blocks(units, 8, C)],
-        out_shape=[
-            triples(chunks, 9),
-            jax.ShapeDtypeStruct((chunks, D, C), BF16),
-            jax.ShapeDtypeStruct((chunks, 8, C), F32),
-        ],
+        out_specs=blocks(units, 10, C, 2 * D),
+        out_shape=triples(chunks, 10),
         compiler_params=params(),
         cost_estimate=cost(20_000_000_000, 20_000_000),
         name="key_maps",
@@ -423,20 +429,20 @@
     )(starts, base, maps, v, maps, v)
 
 
-def run_queries(q, kt, maps, rows, zf, zb, units=16):
+def run_queries(q, maps, zf, zb, units=16):
     chunks = q.shape[0]
     return pl.pallas_call(
         functools.partial(query_kernel, units),
         grid=(chunks // units,),
-        in_specs=[blocks(units, C, D), blocks(units, D, C)]
-        + [blocks(units, 3, C, 2 * D, group=2), blocks(units, 8, C)]
+        in_specs=[blocks(units, C, D)]
+        + [blocks(units, 3, C, 2 * D, group=2), blocks(units, 1, C, 2 * D, group=9)]
         + [blocks(units, 3, C, 2 * D)] * 2,
         out_specs=blocks(units, 3, C, 2 * D),
         out_shape=triples(chunks),
         compiler_params=params(36),
         cost_estimate=cost(20_000_000_000, 20_000_000),
         name="local_out",
-    )(q, kt, maps, rows, zf, zb)
+    )(q, maps, maps, zf, zb)
 
 
 def run_final(starts, base, f, arrived, units=16):
@@ -469,12 +475,12 @@
     kmsg = spread(pack(keys, (beta.T, log_decay.T)))
     v = spread(pack(values))
     q = spread(pack(queries))
-    maps, kt, rows = run_keys(starts, base, kmsg)
+    maps = run_keys(starts, base, kmsg)
     zf, zb, total = run_scan(starts, base, v, maps)
     arrived = [
         lax.ppermute(total, "x", [(i, (i + d) % groups) for i in range(groups)]) for d in (1, 2, 3)
     ]
-    f = run_queries(q, kt, maps, rows, zf, zb)
+    f = run_queries(q, maps, zf, zb)
     return unpack(spread(run_final(starts, base, f, arrived)))
 
 

time: 115 us -> 113 us (0.983)
  Pallas kernels: 46.9 us -> 45.7 us
    unnamed x8 -> x4, local copies, waits for them, and re-layouts: 3.7 us -> 2.79 us
where the time goes in v4:
time: 113 us; the launch traced here: 112 us
  Pallas kernels  45.7 us (40%)
  blocking collectives  23.9 us (21%)
  starting transfers between devices  22.2 us (20%)
  waiting for transfers between devices  17.5 us (15%)
  local copies, waits for them, and re-layouts  2.79 us (2%)
    all_to_all x1, blocking collectives, spread(): return lax.all_to_all(array, GROUP, split_axis=0, concat_axis=0, tiled=True)  23.9 us
    all_to_all x3, starting transfers between devices, spread(): return lax.all_to_all(array, GROUP, split_axis=0, concat_axis=0, tiled=True)  18.6 us
    all_to_all x3, waiting for transfers between devices, spread(): return lax.all_to_all(array, GROUP, split_axis=0, concat_axis=0, tiled=True)  17.4 us
    pallas_call x1, Pallas kernels, run_keys(): pl.pallas_call(functools.partial(key_kernel, units), grid=(chunks // unit...  14.6 us
    pallas_call x1, Pallas kernels, run_scan(): pl.pallas_call(functools.partial(scan_kernel, units, chunks), grid=(n,),...  12.2 us
    pallas_call x1, Pallas kernels, run_queries(): pl.pallas_call(functools.partial(query_kernel, units), grid=(chunks // un...  8.8 us
    pallas_call x3, Pallas kernels, pack(): pl.pallas_call(pack_kernel if extra is None else pack_extra_kernel, grid=...  6.4 us
    ppermute x3, starting transfers between devices, on_device(): lax.ppermute(total, 'x', [(i, (i + d) % groups) for i in range(groups)])  3.61 us
  transfers between devices with their start and end apart: 6, of which 3 were waited for; matrix products, arithmetic and copies ran while one was open for 0% of the time, Pallas kernels for 35%

profile of v4, /device:TPU:1, one launch (start us, length us, event | category | flops | bytes accessed | tf_op | source)
XLA Modules:
  0.0 112.2 jit_solution(12883077544145473258)
XLA Ops:
  0.0 2.2 %pack.4 = bf16[32,144,128]{2,1,0:T(8,128)(2,1)} custom-call(bf16[128,4096]{1,0:T(8,128)(2,1)} %src_ref.4, bf16[32,128]{1,0:T(8,128)(2,1)} %bitcast.3, bf16[32,128]{1,0:T(8,128)(2,1)} %bitcast.4), custom_call_target="tpu_custom_call" | custom-call | bytes 4000000 | tf_op jit(solution)/shard_map/pack/pallas_call | solution.py:368
  2.2 9.6 %all-to-all-start.1 = ((bf16[32,144,128]{2,1,0:T(8,128)(2,1)}), bf16[32,144,128]{2,1,0:T(8,128)(2,1)S(1)}, u32[]{:S(2)}, u32[]{:S(2)}) async-start(bf16[32,144,128]{2,1,0:T(8,128)(2,1)} %pack.4), calls=%async_computation.1 | async-start | bytes 2359296 | tf_op jit(solution)/shard_map/all_to_all | solution.py:465
  11.8 2.1 %pack.3 = bf16[32,128,128]{2,1,0:T(8,128)(2,1)} custom-call(bf16[128,4096]{1,0:T(8,128)(2,1)} %src_ref.3), custom_call_target="tpu_custom_call" | custom-call | bytes 4000000 | tf_op jit(solution)/shard_map/pack/pallas_call | solution.py:368
  13.9 2.1 %pack.5 = bf16[32,128,128]{2,1,0:T(8,128)(2,1)} custom-call(bf16[128,4096]{1,0:T(8,128)(2,1)} %src_ref.5), custom_call_target="tpu_custom_call" | custom-call | bytes 4000000 | tf_op jit(solution)/shard_map/pack/pallas_call | solution.py:368
  16.0 0.0 copy-done.1
  16.0 0.1 select_reduce_fusion.starts_ref
  16.1 14.0 %all-to-all-done.1.kmsg_ref = bf16[32,144,128]{2,1,0:T(8,128)(2,1)S(1)} async-done(((bf16[32,144,128]{2,1,0:T(8,128)(2,1)}), bf16[32,144,128]{2,1,0:T(8,128)(2,1)S(1)}, u32[]{:S(2)}, u32[]{:S(2)}) %all-to-all-start.1) | async-done | bytes 1179680 | tf_op jit(solution)/shard_map/all_to_all | solution.py:465
  30.2 3.9 %all-to-all-start.2 = ((bf16[32,128,128]{2,1,0:T(8,128)(2,1)}), bf16[32,128,128]{2,1,0:T(8,128)(2,1)S(1)}, u32[]{:S(2)}, u32[]{:S(2)}) async-start(bf16[32,128,128]{2,1,0:T(8,128)(2,1)} %pack.5), calls=%async_computation.2 | async-start | bytes 2097152 | tf_op jit(solution)/shard_map/all_to_all | solution.py:465
  34.1 14.6 %key_maps.1.ff_ref.bb_ref.maps_ref.more_ref = bf16[32,10,128,256]{3,2,1,0:T(8,128)(2,1)} custom-call(s32[8]{0:T(128)S(1)} %select_reduce_fusion.starts_ref, s32[1]{0:T(128)} %bitcast.base_ref, bf16[32,144,128]{2,1,0:T(8,128)(2,1)S(1)} %all-to-all-done.1.kmsg_ref), custom_call_target="tpu_custom_call" | custom-call | flops 20000000000 | bytes 20000000 | tf_op jit(solution)/shard_map/key_maps/pallas_call | solution.py:401
  48.7 2.3 %all-to-all-done.2.vf_ref.vb_ref = bf16[32,128,128]{2,1,0:T(8,128)(2,1)S(1)} async-done(((bf16[32,128,128]{2,1,0:T(8,128)(2,1)}), bf16[32,128,128]{2,1,0:T(8,128)(2,1)S(1)}, u32[]{:S(2)}, u32[]{:S(2)}) %all-to-all-start.2) | async-done | bytes 1048608 | tf_op jit(solution)/shard_map/all_to_all | solution.py:465
  51.0 5.1 %all-to-all-start = ((bf16[32,128,128]{2,1,0:T(8,128)(2,1)}), bf16[32,128,128]{2,1,0:T(8,128)(2,1)S(1)}, u32[]{:S(2)}, u32[]{:S(2)}) async-start(bf16[32,128,128]{2,1,0:T(8,128)(2,1)} %pack.3), calls=%async_computation | async-start | bytes 2097152 | tf_op jit(solution)/shard_map/all_to_all | solution.py:465
  56.1 12.2 %scan.1 = (bf16[32,3,128,256]{3,2,1,0:T(8,128)(2,1)}, bf16[32,3,128,256]{3,2,1,0:T(8,128)(2,1)}, f32[3,128,128]{2,1,0:T(8,128)S(1)}) custom-call(s32[8]{0:T(128)S(1)} %select_reduce_fusion.starts_ref, s32[1]{0:T(128)} %bitcast.base_ref, bf16[32,10,128,256]{3,2,1,0:T(8,128)(2,1)} %key_maps.1.ff_ref.bb_ref.maps_ref.more_ref, ...), custom_call_target="tpu_custom_call" | custom-call | flops 20000000000 | bytes 20000000 | tf_op jit(solution)/shard_map/scan/pallas_call | solution.py:416
  68.3 2.5 %collective-permute-start.2 = (f32[3,128,128]{2,1,0:T(8,128)S(1)}, f32[3,128,128]{2,1,0:T(8,128)S(1)}, u32[]{:S(2)}, u32[]{:S(2)}) collective-permute-start(f32[3,128,128]{2,1,0:T(8,128)S(1)} %get-tuple-element.10), channel_id=1, source_target_pairs={{0,96},{32,0},{64,32},{96,64},{1,97},{33,1},{65,33},{97,65},{2,98}... | collective-permute-start | bytes 589832 | tf_op jit(solution)/shard_map/ppermute | solution.py:481
  70.8 0.5 collective-permute-start.1
  71.3 0.6 collective-permute-start
  71.9 1.1 all-to-all-done.q_ref
  73.0 2.8 %copy-done = bf16[32,3,128,256]{3,2,1,0:T(8,128)(2,1)S(1)} copy-done((bf16[32,3,128,256]{3,2,1,0:T(8,128)(2,1)S(1)}, bf16[32,3,128,256]{3,2,1,0:T(8,128)(2,1)}, u32[]{:S(2)}) %copy-start) | copy-done | bytes 6291480
  75.8 8.8 %local_out.1.f_ref = bf16[32,3,128,256]{3,2,1,0:T(8,128)(2,1)S(1)} custom-call(bf16[32,128,128]{2,1,0:T(8,128)(2,1)S(1)} %all-to-all-done.q_ref, bf16[32,10,128,256]{3,2,1,0:T(8,128)(2,1)} %key_maps.1.ff_ref.bb_ref.maps_ref.more_ref, bf16[32,10,128,256]{3,2,1,0:T(8,128)(2,1)} %key_maps.1.ff_ref.bb_ref.maps_ref.more_ref, ...), custom_call_target="tpu_custom_call" | custom-call | flops 20000000000 | bytes 20000000 | tf_op jit(solution)/shard_map/local_out/pallas_call | solution.py:434
  84.6 0.0 collective-permute-done.2.three_ref
  84.6 0.0 collective-permute-done.1.two_ref
  84.6 0.0 collective-permute-done.one_ref
  84.6 2.6 %final.1 = bf16[32,128,128]{2,1,0:T(8,128)(2,1)S(1)} custom-call(s32[8]{0:T(128)S(1)} %select_reduce_fusion.starts_ref, s32[1]{0:T(128)} %bitcast.base_ref, bf16[32,3,128,256]{3,2,1,0:T(8,128)(2,1)S(1)} %local_out.1.f_ref, f32[3,128,128]{2,1,0:T(8,128)S(1)} %collective-permute-done.one_ref, f32[3,128,128]{2,1,0:T(8,128)S(1)} %collective-permute-done.1.two_ref, ...), custom_call_target="tpu_custom_call" | custom-call | flops 2000000000 | bytes 10000000 | tf_op jit(solution)/shard_map/final/pallas_call | solution.py:451
  87.2 23.9 %all_to_all.20.src_ref = bf16[32,128,128]{2,1,0:T(8,128)(2,1)S(1)} all-to-all(bf16[32,128,128]{2,1,0:T(8,128)(2,1)S(1)} %final.1), channel_id=1, replica_groups=mesh['x'=4,'y'=4,'z'=4,'core'=2] {'y','z','core'}, dimensions={0} | all-to-all | bytes 2097152 | tf_op jit(solution)/shard_map/all_to_all | solution.py:465
  111.1 1.1 unpack.1
  (2 shorter events, 0.0 us)
Async XLA Ops:
  0.0 16.0 %copy-start.1 = (s32[8]{0:T(128)S(1)}, s32[8]{0:T(128)}, u32[]{:S(2)}) copy-start(s32[8]{0:T(128)} %param.11) | copy-start | bytes 100
  2.2 28.0 %all-to-all-start.1 = ((bf16[32,144,128]{2,1,0:T(8,128)(2,1)}), bf16[32,144,128]{2,1,0:T(8,128)(2,1)S(1)}, u32[]{:S(2)}, u32[]{:S(2)}) async-start(bf16[32,144,128]{2,1,0:T(8,128)(2,1)} %pack.4), calls=%async_computation.1 | async-start | bytes 2359296 | tf_op jit(solution)/shard_map/all_to_all | solution.py:465
  30.2 20.8 %all-to-all-start.2 = ((bf16[32,128,128]{2,1,0:T(8,128)(2,1)}), bf16[32,128,128]{2,1,0:T(8,128)(2,1)S(1)}, u32[]{:S(2)}, u32[]{:S(2)}) async-start(bf16[32,128,128]{2,1,0:T(8,128)(2,1)} %pack.5), calls=%async_computation.2 | async-start | bytes 2097152 | tf_op jit(solution)/shard_map/all_to_all | solution.py:465
  51.0 22.0 %all-to-all-start = ((bf16[32,128,128]{2,1,0:T(8,128)(2,1)}), bf16[32,128,128]{2,1,0:T(8,128)(2,1)S(1)}, u32[]{:S(2)}, u32[]{:S(2)}) async-start(bf16[32,128,128]{2,1,0:T(8,128)(2,1)} %pack.3), calls=%async_computation | async-start | bytes 2097152 | tf_op jit(solution)/shard_map/all_to_all | solution.py:465
  68.3 16.3 %collective-permute-start.2 = (f32[3,128,128]{2,1,0:T(8,128)S(1)}, f32[3,128,128]{2,1,0:T(8,128)S(1)}, u32[]{:S(2)}, u32[]{:S(2)}) collective-permute-start(f32[3,128,128]{2,1,0:T(8,128)S(1)} %get-tuple-element.10), channel_id=1, source_target_pairs={{0,96},{32,0},{64,32},{96,64},{1,97},{33,1},{65,33},{97,65},{2,98}... | collective-permute-start | bytes 589832 | tf_op jit(solution)/shard_map/ppermute | solution.py:481
  70.8 13.8 %collective-permute-start.1 = (f32[3,128,128]{2,1,0:T(8,128)S(1)}, f32[3,128,128]{2,1,0:T(8,128)S(1)}, u32[]{:S(2)}, u32[]{:S(2)}) collective-permute-start(f32[3,128,128]{2,1,0:T(8,128)S(1)} %get-tuple-element.10), channel_id=1, source_target_pairs={{0,64},{32,96},{64,0},{96,32},{1,65},{33,97},{65,1},{97,33},{2,66}... | collective-permute-start | bytes 589832 | tf_op jit(solution)/shard_map/ppermute | solution.py:481
  71.3 13.3 %collective-permute-start = (f32[3,128,128]{2,1,0:T(8,128)S(1)}, f32[3,128,128]{2,1,0:T(8,128)S(1)}, u32[]{:S(2)}, u32[]{:S(2)}) collective-permute-start(f32[3,128,128]{2,1,0:T(8,128)S(1)} %get-tuple-element.10), channel_id=1, source_target_pairs={{0,32},{32,64},{64,96},{96,0},{1,33},{33,65},{65,97},{97,1},{2,34}... | collective-permute-start | bytes 589832 | tf_op jit(solution)/shard_map/ppermute | solution.py:481
  73.0 2.8 %copy-start = (bf16[32,3,128,256]{3,2,1,0:T(8,128)(2,1)S(1)}, bf16[32,3,128,256]{3,2,1,0:T(8,128)(2,1)}, u32[]{:S(2)}) copy-start(bf16[32,3,128,256]{3,2,1,0:T(8,128)(2,1)} %get-tuple-element.8.zf_ref) | copy-start | bytes 18874372

commit v5 on v4

--- a/solution.py
+++ b/solution.py
@@ -439,7 +439,7 @@
         + [blocks(units, 3, C, 2 * D)] * 2,
         out_specs=blocks(units, 3, C, 2 * D),
         out_shape=triples(chunks),
-        compiler_params=params(36),
+        compiler_params=params(43),
         cost_estimate=cost(20_000_000_000, 20_000_000),
         name="local_out",
     )(q, maps, maps, zf, zb)
@@ -455,7 +455,7 @@
         out_specs=blocks(units, C, D),
         out_shape=jax.ShapeDtypeStruct((chunks, C, D), BF16),
         scratch_shapes=[pltpu.VMEM((2 * D, 2 * D), BF16)],
-        compiler_params=params(36),
+        compiler_params=params(43),
         cost_estimate=cost(2_000_000_000, 10_000_000),
         name="final",
     )(starts, base, f, *arrived)

time: 113 us -> 112 us (level)
  local copies, waits for them, and re-layouts: 2.79 us -> 0.01 us
    unnamed x4 -> x2, local copies, waits for them, and re-layouts: 2.79 us -> 0.01 us
  transfers between devices with their start and end apart: 6 -> 6, of which waited for: 3 -> 4; matrix products, arithmetic and copies ran while one was open for 0% -> 0% of each run, Pallas kernels for 35% -> 37%
where the time goes in v5:
time: 112 us; the launch traced here: 111 us
  Pallas kernels  46.7 us (42%)
  blocking collectives  24.2 us (22%)
  starting transfers between devices  22.2 us (20%)
  waiting for transfers between devices  17.9 us (16%)
    all_to_all x1, blocking collectives, spread(): return lax.all_to_all(array, GROUP, split_axis=0, concat_axis=0, tiled=True)  24.2 us
    all_to_all x3, starting transfers between devices, spread(): return lax.all_to_all(array, GROUP, split_axis=0, concat_axis=0, tiled=True)  18.6 us
    all_to_all x3, waiting for transfers between devices, spread(): return lax.all_to_all(array, GROUP, split_axis=0, concat_axis=0, tiled=True)  17.5 us
    pallas_call x1, Pallas kernels, run_keys(): pl.pallas_call(functools.partial(key_kernel, units), grid=(chunks // unit...  14.6 us
    pallas_call x1, Pallas kernels, run_scan(): pl.pallas_call(functools.partial(scan_kernel, units, chunks), grid=(n,),...  12.2 us
    pallas_call x1, Pallas kernels, run_queries(): pl.pallas_call(functools.partial(query_kernel, units), grid=(chunks // un...  9.86 us
    pallas_call x3, Pallas kernels, pack(): pl.pallas_call(pack_kernel if extra is None else pack_extra_kernel, grid=...  6.41 us
    ppermute x3, starting transfers between devices, on_device(): lax.ppermute(total, 'x', [(i, (i + d) % groups) for i in range(groups)])  3.59 us
  transfers between devices with their start and end apart: 6, of which 4 were waited for; matrix products, arithmetic and copies ran while one was open for 0% of the time, Pallas kernels for 37%

profile of v5, /device:TPU:1, one launch (start us, length us, event | category | flops | bytes accessed | tf_op | source)
XLA Modules:
  0.0 111.2 jit_solution(10335598111861238891)
XLA Ops:
  0.0 0.0 copy-start
  0.0 2.2 %pack.4 = bf16[32,144,128]{2,1,0:T(8,128)(2,1)} custom-call(bf16[128,4096]{1,0:T(8,128)(2,1)} %src_ref.4, bf16[32,128]{1,0:T(8,128)(2,1)} %bitcast.3, bf16[32,128]{1,0:T(8,128)(2,1)} %bitcast.4), custom_call_target="tpu_custom_call" | custom-call | bytes 4000000 | tf_op jit(solution)/shard_map/pack/pallas_call | solution.py:368
  2.2 9.6 %all-to-all-start.1 = ((bf16[32,144,128]{2,1,0:T(8,128)(2,1)}), bf16[32,144,128]{2,1,0:T(8,128)(2,1)S(1)}, u32[]{:S(2)}, u32[]{:S(2)}) async-start(bf16[32,144,128]{2,1,0:T(8,128)(2,1)} %pack.4), calls=%async_computation.1 | async-start | bytes 2359296 | tf_op jit(solution)/shard_map/all_to_all | solution.py:465
  11.8 2.1 %pack.3 = bf16[32,128,128]{2,1,0:T(8,128)(2,1)} custom-call(bf16[128,4096]{1,0:T(8,128)(2,1)} %src_ref.3), custom_call_target="tpu_custom_call" | custom-call | bytes 4000000 | tf_op jit(solution)/shard_map/pack/pallas_call | solution.py:368
  13.9 2.1 %pack.5 = bf16[32,128,128]{2,1,0:T(8,128)(2,1)} custom-call(bf16[128,4096]{1,0:T(8,128)(2,1)} %src_ref.5), custom_call_target="tpu_custom_call" | custom-call | bytes 4000000 | tf_op jit(solution)/shard_map/pack/pallas_call | solution.py:368
  16.0 0.0 copy-done
  16.0 0.1 select_reduce_fusion.starts_ref
  16.2 14.0 %all-to-all-done.1.kmsg_ref = bf16[32,144,128]{2,1,0:T(8,128)(2,1)S(1)} async-done(((bf16[32,144,128]{2,1,0:T(8,128)(2,1)}), bf16[32,144,128]{2,1,0:T(8,128)(2,1)S(1)}, u32[]{:S(2)}, u32[]{:S(2)}) %all-to-all-start.1) | async-done | bytes 1179680 | tf_op jit(solution)/shard_map/all_to_all | solution.py:465
  30.2 3.9 %all-to-all-start.2 = ((bf16[32,128,128]{2,1,0:T(8,128)(2,1)}), bf16[32,128,128]{2,1,0:T(8,128)(2,1)S(1)}, u32[]{:S(2)}, u32[]{:S(2)}) async-start(bf16[32,128,128]{2,1,0:T(8,128)(2,1)} %pack.5), calls=%async_computation.2 | async-start | bytes 2097152 | tf_op jit(solution)/shard_map/all_to_all | solution.py:465
  34.1 14.6 %key_maps.1.ff_ref.bb_ref.maps_ref.more_ref = bf16[32,10,128,256]{3,2,1,0:T(8,128)(2,1)} custom-call(s32[8]{0:T(128)S(1)} %select_reduce_fusion.starts_ref, s32[1]{0:T(128)} %bitcast.base_ref, bf16[32,144,128]{2,1,0:T(8,128)(2,1)S(1)} %all-to-all-done.1.kmsg_ref), custom_call_target="tpu_custom_call" | custom-call | flops 20000000000 | bytes 20000000 | tf_op jit(solution)/shard_map/key_maps/pallas_call | solution.py:401
  48.7 2.4 %all-to-all-done.2.vf_ref.vb_ref = bf16[32,128,128]{2,1,0:T(8,128)(2,1)S(1)} async-done(((bf16[32,128,128]{2,1,0:T(8,128)(2,1)}), bf16[32,128,128]{2,1,0:T(8,128)(2,1)S(1)}, u32[]{:S(2)}, u32[]{:S(2)}) %all-to-all-start.2) | async-done | bytes 1048608 | tf_op jit(solution)/shard_map/all_to_all | solution.py:465
  51.0 5.1 %all-to-all-start = ((bf16[32,128,128]{2,1,0:T(8,128)(2,1)}), bf16[32,128,128]{2,1,0:T(8,128)(2,1)S(1)}, u32[]{:S(2)}, u32[]{:S(2)}) async-start(bf16[32,128,128]{2,1,0:T(8,128)(2,1)} %pack.3), calls=%async_computation | async-start | bytes 2097152 | tf_op jit(solution)/shard_map/all_to_all | solution.py:465
  56.1 12.2 %scan.1 = (bf16[32,3,128,256]{3,2,1,0:T(8,128)(2,1)}, bf16[32,3,128,256]{3,2,1,0:T(8,128)(2,1)}, f32[3,128,128]{2,1,0:T(8,128)S(1)}) custom-call(s32[8]{0:T(128)S(1)} %select_reduce_fusion.starts_ref, s32[1]{0:T(128)} %bitcast.base_ref, bf16[32,10,128,256]{3,2,1,0:T(8,128)(2,1)} %key_maps.1.ff_ref.bb_ref.maps_ref.more_ref, ...), custom_call_target="tpu_custom_call" | custom-call | flops 20000000000 | bytes 20000000 | tf_op jit(solution)/shard_map/scan/pallas_call | solution.py:416
  68.3 2.5 %collective-permute-start.2 = (f32[3,128,128]{2,1,0:T(8,128)S(1)}, f32[3,128,128]{2,1,0:T(8,128)S(1)}, u32[]{:S(2)}, u32[]{:S(2)}) collective-permute-start(f32[3,128,128]{2,1,0:T(8,128)S(1)} %get-tuple-element.10), channel_id=1, source_target_pairs={{0,96},{32,0},{64,32},{96,64},{1,97},{33,1},{65,33},{97,65},{2,98}... | collective-permute-start | bytes 589832 | tf_op jit(solution)/shard_map/ppermute | solution.py:481
  70.8 0.5 collective-permute-start.1
  71.3 0.6 collective-permute-start
  71.9 1.1 %all-to-all-done.q_ref = bf16[32,128,128]{2,1,0:T(8,128)(2,1)S(1)} async-done(((bf16[32,128,128]{2,1,0:T(8,128)(2,1)}), bf16[32,128,128]{2,1,0:T(8,128)(2,1)S(1)}, u32[]{:S(2)}, u32[]{:S(2)}) %all-to-all-start) | async-done | bytes 1048608 | tf_op jit(solution)/shard_map/all_to_all | solution.py:465
  73.0 9.9 %local_out.1.f_ref = bf16[32,3,128,256]{3,2,1,0:T(8,128)(2,1)S(1)} custom-call(bf16[32,128,128]{2,1,0:T(8,128)(2,1)S(1)} %all-to-all-done.q_ref, bf16[32,10,128,256]{3,2,1,0:T(8,128)(2,1)} %key_maps.1.ff_ref.bb_ref.maps_ref.more_ref, bf16[32,10,128,256]{3,2,1,0:T(8,128)(2,1)} %key_maps.1.ff_ref.bb_ref.maps_ref.more_ref, ...), custom_call_target="tpu_custom_call" | custom-call | flops 20000000000 | bytes 20000000 | tf_op jit(solution)/shard_map/local_out/pallas_call | solution.py:434
  82.9 0.0 collective-permute-done.2.three_ref
  82.9 0.0 collective-permute-done.1.two_ref
  82.9 0.4 collective-permute-done.one_ref
  83.3 2.6 %final.1 = bf16[32,128,128]{2,1,0:T(8,128)(2,1)S(1)} custom-call(s32[8]{0:T(128)S(1)} %select_reduce_fusion.starts_ref, s32[1]{0:T(128)} %bitcast.base_ref, bf16[32,3,128,256]{3,2,1,0:T(8,128)(2,1)S(1)} %local_out.1.f_ref, f32[3,128,128]{2,1,0:T(8,128)S(1)} %collective-permute-done.one_ref, f32[3,128,128]{2,1,0:T(8,128)S(1)} %collective-permute-done.1.two_ref, ...), custom_call_target="tpu_custom_call" | custom-call | flops 2000000000 | bytes 10000000 | tf_op jit(solution)/shard_map/final/pallas_call | solution.py:451
  85.9 24.2 %all_to_all.20.src_ref = bf16[32,128,128]{2,1,0:T(8,128)(2,1)S(1)} all-to-all(bf16[32,128,128]{2,1,0:T(8,128)(2,1)S(1)} %final.1), channel_id=1, replica_groups=mesh['x'=4,'y'=4,'z'=4,'core'=2] {'y','z','core'}, dimensions={0} | all-to-all | bytes 2097152 | tf_op jit(solution)/shard_map/all_to_all | solution.py:465
  110.1 1.1 unpack.1
Async XLA Ops:
  0.0 16.0 %copy-start = (s32[8]{0:T(128)S(1)}, s32[8]{0:T(128)}, u32[]{:S(2)}) copy-start(s32[8]{0:T(128)} %param.11) | copy-start | bytes 100
  2.2 28.0 %all-to-all-start.1 = ((bf16[32,144,128]{2,1,0:T(8,128)(2,1)}), bf16[32,144,128]{2,1,0:T(8,128)(2,1)S(1)}, u32[]{:S(2)}, u32[]{:S(2)}) async-start(bf16[32,144,128]{2,1,0:T(8,128)(2,1)} %pack.4), calls=%async_computation.1 | async-start | bytes 2359296 | tf_op jit(solution)/shard_map/all_to_all | solution.py:465
  30.2 20.8 %all-to-all-start.2 = ((bf16[32,128,128]{2,1,0:T(8,128)(2,1)}), bf16[32,128,128]{2,1,0:T(8,128)(2,1)S(1)}, u32[]{:S(2)}, u32[]{:S(2)}) async-start(bf16[32,128,128]{2,1,0:T(8,128)(2,1)} %pack.5), calls=%async_computation.2 | async-start | bytes 2097152 | tf_op jit(solution)/shard_map/all_to_all | solution.py:465
  51.0 22.0 %all-to-all-start = ((bf16[32,128,128]{2,1,0:T(8,128)(2,1)}), bf16[32,128,128]{2,1,0:T(8,128)(2,1)S(1)}, u32[]{:S(2)}, u32[]{:S(2)}) async-start(bf16[32,128,128]{2,1,0:T(8,128)(2,1)} %pack.3), calls=%async_computation | async-start | bytes 2097152 | tf_op jit(solution)/shard_map/all_to_all | solution.py:465
  68.3 14.6 %collective-permute-start.2 = (f32[3,128,128]{2,1,0:T(8,128)S(1)}, f32[3,128,128]{2,1,0:T(8,128)S(1)}, u32[]{:S(2)}, u32[]{:S(2)}) collective-permute-start(f32[3,128,128]{2,1,0:T(8,128)S(1)} %get-tuple-element.10), channel_id=1, source_target_pairs={{0,96},{32,0},{64,32},{96,64},{1,97},{33,1},{65,33},{97,65},{2,98}... | collective-permute-start | bytes 589832 | tf_op jit(solution)/shard_map/ppermute | solution.py:481
  70.8 12.1 %collective-permute-start.1 = (f32[3,128,128]{2,1,0:T(8,128)S(1)}, f32[3,128,128]{2,1,0:T(8,128)S(1)}, u32[]{:S(2)}, u32[]{:S(2)}) collective-permute-start(f32[3,128,128]{2,1,0:T(8,128)S(1)} %get-tuple-element.10), channel_id=1, source_target_pairs={{0,64},{32,96},{64,0},{96,32},{1,65},{33,97},{65,1},{97,33},{2,66}... | collective-permute-start | bytes 589832 | tf_op jit(solution)/shard_map/ppermute | solution.py:481
  71.3 12.0 %collective-permute-start = (f32[3,128,128]{2,1,0:T(8,128)S(1)}, f32[3,128,128]{2,1,0:T(8,128)S(1)}, u32[]{:S(2)}, u32[]{:S(2)}) collective-permute-start(f32[3,128,128]{2,1,0:T(8,128)S(1)} %get-tuple-element.10), channel_id=1, source_target_pairs={{0,32},{32,64},{64,96},{96,0},{1,33},{33,65},{65,97},{97,1},{2,34}... | collective-permute-start | bytes 589832 | tf_op jit(solution)/shard_map/ppermute | solution.py:481

commit v6 on v5

--- a/solution.py
+++ b/solution.py
@@ -193,7 +193,7 @@
 
 def scan_kernel(
     units, chunks, starts_ref, base_ref, ff_ref, vf_ref, bb_ref, vb_ref,
-    zf_ref, zb_ref, total_ref, forward, backward,
+    zf_ref, zb_ref, one_ref, two_ref, three_ref, forward, backward,
 ):
     step = pl.program_id(0)
 
@@ -247,9 +247,10 @@
         zb = zb + beyond(inject_b[r])
     forward[...] = zf
     backward[...] = zb
-    total_ref[0] = zf[:, D:]
-    total_ref[1] = zf[:, :D]
-    total_ref[2] = zb[:, :D]
+    mine = base_ref[0] // (chunks * C)
+    for d, total_ref in ((1, one_ref), (2, two_ref), (3, three_ref)):
+        total_ref[0] = zf[:, D:]
+        total_ref[1] = jnp.where(mine + d < 4, zf[:, :D], zb[:, :D])
 
 
 def query_kernel(units, q_ref, maps_ref, more_ref, zf_ref, zb_ref, f_ref):
@@ -307,7 +308,7 @@
             moved = dot3(arrived[e][0], sf * keep(cut)) + arrived[e][1]
             sf = jnp.where(e <= mine, moved, sf)
             cut = is_start(starts_ref, (mine - d + 5) * span)
-            moved = dot3(turned[d], sb * keep(cut)) + arrived[d][2]
+            moved = dot3(turned[d], sb * keep(cut)) + arrived[d][1]
             sb = jnp.where(d > mine, moved, sb)
         sf = sf * keep(is_start(starts_ref, mine * span))
         sb = sb * keep(is_start(starts_ref, (mine + 1) * span))
@@ -420,8 +421,8 @@
         + [blocks(units, 3, C, 2 * D), blocks(units, C, D)]
         + [blocks(units, 3, C, 2 * D, flip=n, group=1), blocks(units, C, D, flip=n)],
         out_specs=[blocks(units, 3, C, 2 * D), blocks(units, 3, C, 2 * D, flip=n)]
-        + [pl.BlockSpec((3, D, D), lambda i: (0, 0, 0))],
-        out_shape=[triples(chunks)] * 2 + [jax.ShapeDtypeStruct((3, D, D), F32)],
+        + [pl.BlockSpec((2, D, D), lambda i: (0, 0, 0))] * 3,
+        out_shape=[triples(chunks)] * 2 + [jax.ShapeDtypeStruct((2, D, D), F32)] * 3,
         scratch_shapes=[pltpu.VMEM((D, 2 * D), F32)] * 2,
         compiler_params=params(),
         cost_estimate=cost(20_000_000_000, 20_000_000),
@@ -447,7 +448,7 @@
 
 def run_final(starts, base, f, arrived, units=16):
     chunks = f.shape[0]
-    whole = pl.BlockSpec((3, D, D), lambda i: (0, 0, 0))
+    whole = pl.BlockSpec((2, D, D), lambda i: (0, 0, 0))
     return pl.pallas_call(
         functools.partial(final_kernel, units, chunks * C),
         grid=(chunks // units,),
@@ -476,9 +477,10 @@
     v = spread(pack(values))
     q = spread(pack(queries))
     maps = run_keys(starts, base, kmsg)
-    zf, zb, total = run_scan(starts, base, v, maps)
+    zf, zb, *totals = run_scan(starts, base, v, maps)
     arrived = [
-        lax.ppermute(total, "x", [(i, (i + d) % groups) for i in range(groups)]) for d in (1, 2, 3)
+        lax.ppermute(totals[d - 1], "x", [(i, (i + d) % groups) for i in range(groups)])
+        for d in (1, 2, 3)
     ]
     f = run_queries(q, maps, zf, zb)
     return unpack(spread(run_final(starts, base, f, arrived)))

time: 112 us -> 112 us (level)
  waiting for transfers between devices: 17.9 us -> 16.4 us
  starting transfers between devices: 22.2 us -> 23.4 us
    ppermute x3, starting transfers between devices: 3.59 us -> 4.8 us  [on_device(): lax.ppermute(totals[d - 1], 'x', [(i, (i + d) % groups) for i in range(gr...]
  transfers between devices with their start and end apart: 6 -> 6, of which waited for: 4 -> 2; matrix products, arithmetic and copies ran while one was open for 0% -> 0% of each run, Pallas kernels for 37% -> 37%
where the time goes in v6:
time: 112 us
  Pallas kernels  46.7 us (42%)
  blocking collectives  24.9 us (22%)
  starting transfers between devices  23.4 us (21%)
  waiting for transfers between devices  16.4 us (15%)
    all_to_all x1, blocking collectives, spread(): return lax.all_to_all(array, GROUP, split_axis=0, concat_axis=0, tiled=True)  24.9 us
    all_to_all x3, starting transfers between devices, spread(): return lax.all_to_all(array, GROUP, split_axis=0, concat_axis=0, tiled=True)  18.6 us
    all_to_all x3, waiting for transfers between devices, spread(): return lax.all_to_all(array, GROUP, split_axis=0, concat_axis=0, tiled=True)  16.4 us
    pallas_call x1, Pallas kernels, run_keys(): pl.pallas_call(functools.partial(key_kernel, units), grid=(chunks // unit...  14.6 us
    pallas_call x1, Pallas kernels, run_scan(): pl.pallas_call(functools.partial(scan_kernel, units, chunks), grid=(n,),...  12.2 us
    pallas_call x1, Pallas kernels, run_queries(): pl.pallas_call(functools.partial(query_kernel, units), grid=(chunks // un...  9.87 us
    pallas_call x3, Pallas kernels, pack(): pl.pallas_call(pack_kernel if extra is None else pack_extra_kernel, grid=...  6.41 us
    ppermute x3, starting transfers between devices, on_device(): lax.ppermute(totals[d - 1], 'x', [(i, (i + d) % groups) for i in range(gr...  4.8 us
  transfers between devices with their start and end apart: 6, of which 2 were waited for; matrix products, arithmetic and copies ran while one was open for 0% of the time, Pallas kernels for 37%

profile of v6, /device:TPU:1, one launch (start us, length us, event | category | flops | bytes accessed | tf_op | source)
XLA Modules:
  0.0 111.6 jit_solution(13172092469214562462)
XLA Ops:
  0.0 0.0 copy-start
  0.0 2.2 %pack.4 = bf16[32,144,128]{2,1,0:T(8,128)(2,1)} custom-call(bf16[128,4096]{1,0:T(8,128)(2,1)} %src_ref.4, bf16[32,128]{1,0:T(8,128)(2,1)} %bitcast.3, bf16[32,128]{1,0:T(8,128)(2,1)} %bitcast.4), custom_call_target="tpu_custom_call" | custom-call | bytes 4000000 | tf_op jit(solution)/shard_map/pack/pallas_call | solution.py:369
  2.2 9.6 %all-to-all-start.1 = ((bf16[32,144,128]{2,1,0:T(8,128)(2,1)}), bf16[32,144,128]{2,1,0:T(8,128)(2,1)S(1)}, u32[]{:S(2)}, u32[]{:S(2)}) async-start(bf16[32,144,128]{2,1,0:T(8,128)(2,1)} %pack.4), calls=%async_computation.1 | async-start | bytes 2359296 | tf_op jit(solution)/shard_map/all_to_all | solution.py:466
  11.8 2.1 %pack.3 = bf16[32,128,128]{2,1,0:T(8,128)(2,1)} custom-call(bf16[128,4096]{1,0:T(8,128)(2,1)} %src_ref.3), custom_call_target="tpu_custom_call" | custom-call | bytes 4000000 | tf_op jit(solution)/shard_map/pack/pallas_call | solution.py:369
  13.9 2.1 %pack.5 = bf16[32,128,128]{2,1,0:T(8,128)(2,1)} custom-call(bf16[128,4096]{1,0:T(8,128)(2,1)} %src_ref.5), custom_call_target="tpu_custom_call" | custom-call | bytes 4000000 | tf_op jit(solution)/shard_map/pack/pallas_call | solution.py:369
  16.0 0.0 copy-done
  16.0 0.1 select_reduce_fusion.starts_ref
  16.2 14.0 %all-to-all-done.1.kmsg_ref = bf16[32,144,128]{2,1,0:T(8,128)(2,1)S(1)} async-done(((bf16[32,144,128]{2,1,0:T(8,128)(2,1)}), bf16[32,144,128]{2,1,0:T(8,128)(2,1)S(1)}, u32[]{:S(2)}, u32[]{:S(2)}) %all-to-all-start.1) | async-done | bytes 1179680 | tf_op jit(solution)/shard_map/all_to_all | solution.py:466
  30.2 3.9 %all-to-all-start.2 = ((bf16[32,128,128]{2,1,0:T(8,128)(2,1)}), bf16[32,128,128]{2,1,0:T(8,128)(2,1)S(1)}, u32[]{:S(2)}, u32[]{:S(2)}) async-start(bf16[32,128,128]{2,1,0:T(8,128)(2,1)} %pack.5), calls=%async_computation.2 | async-start | bytes 2097152 | tf_op jit(solution)/shard_map/all_to_all | solution.py:466
  34.1 14.6 %key_maps.1.ff_ref.bb_ref.maps_ref.more_ref = bf16[32,10,128,256]{3,2,1,0:T(8,128)(2,1)} custom-call(s32[8]{0:T(128)S(1)} %select_reduce_fusion.starts_ref, s32[1]{0:T(128)} %bitcast.base_ref, bf16[32,144,128]{2,1,0:T(8,128)(2,1)S(1)} %all-to-all-done.1.kmsg_ref), custom_call_target="tpu_custom_call" | custom-call | flops 20000000000 | bytes 20000000 | tf_op jit(solution)/shard_map/key_maps/pallas_call | solution.py:402
  48.7 2.4 %all-to-all-done.2.vf_ref.vb_ref = bf16[32,128,128]{2,1,0:T(8,128)(2,1)S(1)} async-done(((bf16[32,128,128]{2,1,0:T(8,128)(2,1)}), bf16[32,128,128]{2,1,0:T(8,128)(2,1)S(1)}, u32[]{:S(2)}, u32[]{:S(2)}) %all-to-all-start.2) | async-done | bytes 1048608 | tf_op jit(solution)/shard_map/all_to_all | solution.py:466
  51.0 5.1 %all-to-all-start = ((bf16[32,128,128]{2,1,0:T(8,128)(2,1)}), bf16[32,128,128]{2,1,0:T(8,128)(2,1)S(1)}, u32[]{:S(2)}, u32[]{:S(2)}) async-start(bf16[32,128,128]{2,1,0:T(8,128)(2,1)} %pack.3), calls=%async_computation | async-start | bytes 2097152 | tf_op jit(solution)/shard_map/all_to_all | solution.py:466
  56.1 12.2 %scan.1 = (bf16[32,3,128,256]{3,2,1,0:T(8,128)(2,1)}, bf16[32,3,128,256]{3,2,1,0:T(8,128)(2,1)}, f32[2,128,128]{2,1,0:T(8,128)S(1)}, f32[2,128,128]{2,1,0:T(8,128)S(1)}, f32[2,128,128]{2,1,0:T(8,128)S(1)}) custom-call(s32[8]{0:T(128)S(1)} %select_reduce_fusion.starts_ref, s32[1]{0:T(128)} %bitcast.base_ref, ...), custom_call_target="tpu_custom_call" | custom-call | flops 20000000000 | bytes 20000000 | tf_op jit(solution)/shard_map/scan/pallas_call | solution.py:417
  68.3 1.2 %collective-permute-start = (f32[2,128,128]{2,1,0:T(8,128)S(1)}, f32[2,128,128]{2,1,0:T(8,128)S(1)}, u32[]{:S(2)}, u32[]{:S(2)}) collective-permute-start(f32[2,128,128]{2,1,0:T(8,128)S(1)} %get-tuple-element.12), channel_id=1, source_target_pairs={{0,32},{32,64},{64,96},{96,0},{1,33},{33,65},{65,97},{97,1},{2,34}... | collective-permute-start | bytes 393224 | tf_op jit(solution)/shard_map/ppermute | solution.py:482
  69.5 2.4 %collective-permute-start.1 = (f32[2,128,128]{2,1,0:T(8,128)S(1)}, f32[2,128,128]{2,1,0:T(8,128)S(1)}, u32[]{:S(2)}, u32[]{:S(2)}) collective-permute-start(f32[2,128,128]{2,1,0:T(8,128)S(1)} %get-tuple-element.13), channel_id=1, source_target_pairs={{0,64},{32,96},{64,0},{96,32},{1,65},{33,97},{65,1},{97,33},{2,66}... | collective-permute-start | bytes 393224 | tf_op jit(solution)/shard_map/ppermute | solution.py:482
  72.0 1.1 %collective-permute-start.2 = (f32[2,128,128]{2,1,0:T(8,128)S(1)}, f32[2,128,128]{2,1,0:T(8,128)S(1)}, u32[]{:S(2)}, u32[]{:S(2)}) collective-permute-start(f32[2,128,128]{2,1,0:T(8,128)S(1)} %get-tuple-element.14), channel_id=1, source_target_pairs={{0,96},{32,0},{64,32},{96,64},{1,97},{33,1},{65,33},{97,65},{2,98}... | collective-permute-start | bytes 393224 | tf_op jit(solution)/shard_map/ppermute | solution.py:482
  73.1 0.0 all-to-all-done.q_ref
  73.1 9.9 %local_out.1.f_ref = bf16[32,3,128,256]{3,2,1,0:T(8,128)(2,1)S(1)} custom-call(bf16[32,128,128]{2,1,0:T(8,128)(2,1)S(1)} %all-to-all-done.q_ref, bf16[32,10,128,256]{3,2,1,0:T(8,128)(2,1)} %key_maps.1.ff_ref.bb_ref.maps_ref.more_ref, bf16[32,10,128,256]{3,2,1,0:T(8,128)(2,1)} %key_maps.1.ff_ref.bb_ref.maps_ref.more_ref, ...), custom_call_target="tpu_custom_call" | custom-call | flops 20000000000 | bytes 20000000 | tf_op jit(solution)/shard_map/local_out/pallas_call | solution.py:435
  83.0 0.0 collective-permute-done.one_ref
  83.0 0.0 collective-permute-done.1.two_ref
  83.0 0.0 collective-permute-done.2.three_ref
  83.0 2.6 %final.1 = bf16[32,128,128]{2,1,0:T(8,128)(2,1)S(1)} custom-call(s32[8]{0:T(128)S(1)} %select_reduce_fusion.starts_ref, s32[1]{0:T(128)} %bitcast.base_ref, bf16[32,3,128,256]{3,2,1,0:T(8,128)(2,1)S(1)} %local_out.1.f_ref, f32[2,128,128]{2,1,0:T(8,128)S(1)} %collective-permute-done.one_ref, f32[2,128,128]{2,1,0:T(8,128)S(1)} %collective-permute-done.1.two_ref, ...), custom_call_target="tpu_custom_call" | custom-call | flops 2000000000 | bytes 10000000 | tf_op jit(solution)/shard_map/final/pallas_call | solution.py:452
  85.6 24.9 %all_to_all.20.src_ref = bf16[32,128,128]{2,1,0:T(8,128)(2,1)S(1)} all-to-all(bf16[32,128,128]{2,1,0:T(8,128)(2,1)S(1)} %final.1), channel_id=1, replica_groups=mesh['x'=4,'y'=4,'z'=4,'core'=2] {'y','z','core'}, dimensions={0} | all-to-all | bytes 2097152 | tf_op jit(solution)/shard_map/all_to_all | solution.py:466
  110.5 1.1 unpack.1
Async XLA Ops:
  0.0 16.0 %copy-start = (s32[8]{0:T(128)S(1)}, s32[8]{0:T(128)}, u32[]{:S(2)}) copy-start(s32[8]{0:T(128)} %param.11) | copy-start | bytes 100
  2.2 28.0 %all-to-all-start.1 = ((bf16[32,144,128]{2,1,0:T(8,128)(2,1)}), bf16[32,144,128]{2,1,0:T(8,128)(2,1)S(1)}, u32[]{:S(2)}, u32[]{:S(2)}) async-start(bf16[32,144,128]{2,1,0:T(8,128)(2,1)} %pack.4), calls=%async_computation.1 | async-start | bytes 2359296 | tf_op jit(solution)/shard_map/all_to_all | solution.py:466
  30.2 20.8 %all-to-all-start.2 = ((bf16[32,128,128]{2,1,0:T(8,128)(2,1)}), bf16[32,128,128]{2,1,0:T(8,128)(2,1)S(1)}, u32[]{:S(2)}, u32[]{:S(2)}) async-start(bf16[32,128,128]{2,1,0:T(8,128)(2,1)} %pack.5), calls=%async_computation.2 | async-start | bytes 2097152 | tf_op jit(solution)/shard_map/all_to_all | solution.py:466
  51.0 22.1 %all-to-all-start = ((bf16[32,128,128]{2,1,0:T(8,128)(2,1)}), bf16[32,128,128]{2,1,0:T(8,128)(2,1)S(1)}, u32[]{:S(2)}, u32[]{:S(2)}) async-start(bf16[32,128,128]{2,1,0:T(8,128)(2,1)} %pack.3), calls=%async_computation | async-start | bytes 2097152 | tf_op jit(solution)/shard_map/all_to_all | solution.py:466
  68.3 14.7 %collective-permute-start = (f32[2,128,128]{2,1,0:T(8,128)S(1)}, f32[2,128,128]{2,1,0:T(8,128)S(1)}, u32[]{:S(2)}, u32[]{:S(2)}) collective-permute-start(f32[2,128,128]{2,1,0:T(8,128)S(1)} %get-tuple-element.12), channel_id=1, source_target_pairs={{0,32},{32,64},{64,96},{96,0},{1,33},{33,65},{65,97},{97,1},{2,34}... | collective-permute-start | bytes 393224 | tf_op jit(solution)/shard_map/ppermute | solution.py:482
  69.5 13.5 %collective-permute-start.1 = (f32[2,128,128]{2,1,0:T(8,128)S(1)}, f32[2,128,128]{2,1,0:T(8,128)S(1)}, u32[]{:S(2)}, u32[]{:S(2)}) collective-permute-start(f32[2,128,128]{2,1,0:T(8,128)S(1)} %get-tuple-element.13), channel_id=1, source_target_pairs={{0,64},{32,96},{64,0},{96,32},{1,65},{33,97},{65,1},{97,33},{2,66}... | collective-permute-start | bytes 393224 | tf_op jit(solution)/shard_map/ppermute | solution.py:482
  72.0 11.0 %collective-permute-start.2 = (f32[2,128,128]{2,1,0:T(8,128)S(1)}, f32[2,128,128]{2,1,0:T(8,128)S(1)}, u32[]{:S(2)}, u32[]{:S(2)}) collective-permute-start(f32[2,128,128]{2,1,0:T(8,128)S(1)} %get-tuple-element.14), channel_id=1, source_target_pairs={{0,96},{32,0},{64,32},{96,64},{1,97},{33,1},{65,33},{97,65},{2,98}... | collective-permute-start | bytes 393224 | tf_op jit(solution)/shard_map/ppermute | solution.py:482
